TPU v7x, 32 devices: a whole 2x2x4 slice. The times are simulated.
32 devices in a mesh: dp: 8 (over y, x, core), seq: 4 (over z).
Axes of the slice: x: 2, y: 2, z: 4, core: 2. Of those that a mesh axis runs over, the one named last changes fastest.
Arguments:
- pre_activation: bfloat16 [8, 16, 128, 512], P('dp', None, 'seq'), may hold values from -6 to 6
- output_grad: bfloat16 [8, 16, 128, 512], P('dp', None, 'seq'), may hold values from -0.59765625 to 0.59765625
- up_kernel: bfloat16 [3, 3, 512, 512], replicated, may hold values from -0.09375 to 0.09375
- in_kernel: bfloat16 [3, 3, 16, 512], replicated, may hold values from -0.09375 to 0.09375
- final_weight: bfloat16 [64, 3072], replicated, may hold values from -0.75 to 0.75
- gate_table: bfloat16 [8, 3072], replicated, may hold values from -4 to 4
- bucket: int32 [8], P('dp'), may hold values from 0 to 7
- query_vectors: bfloat16 [8, 512, 2048], P('dp', 'seq'), may hold values from -12 to 12
- key_vectors: bfloat16 [8, 512, 2048], P('dp', 'seq'), may hold values from -12 to 12
- value_vectors: bfloat16 [8, 512, 2048], P('dp', 'seq'), may hold values from -6 to 6
- out_weight: bfloat16 [2048, 3072], replicated, may hold values from -1.796875 to 1.796875
- block_input: bfloat16 [8, 512, 3072], P('dp', 'seq'), may hold values from -6 to 6
Outputs:
- query_grad: bfloat16 [8, 512, 2048], P('dp', 'seq')
- key_grad: bfloat16 [8, 512, 2048], P('dp', 'seq')
- value_grad: bfloat16 [8, 512, 2048], P('dp', 'seq')
- weight_grad: float32 [3072, 2048], P(('dp', 'seq'))
All inputs are finite; a program needn't handle non-finite values.
Results may differ from a plain program's by a relative error of at most 0.025.
Values may be sent and summed in bfloat16 or wider, within the bound.
A program may use at most 192 MiB of HBM per device.

v0:
```python
import jax
import jax.numpy as jnp
from jax import lax
from jax.sharding import PartitionSpec as P

DH = 128


def with_halo(block, sides, width):
    for axis, dim in sides:
        count = lax.axis_size(axis)
        forward = [(i, i + 1) for i in range(count - 1)]
        backward = [(target, source) for source, target in forward]
        low = lax.ppermute(
            lax.slice_in_dim(block, block.shape[dim] - width, None, axis=dim), axis, forward
        )
        high = lax.ppermute(lax.slice_in_dim(block, 0, width, axis=dim), axis, backward)
        block = jnp.concatenate([low, block, high], axis=dim)
    return block


def silu_slope(values):
    sigma = jax.nn.sigmoid(values)
    return sigma * (1.0 + values * (1.0 - sigma))


def column_grad(grad, kernel):
    widened = with_halo(grad, (("seq", 2),), 1)
    flipped = jnp.transpose(kernel[::-1, ::-1], (0, 1, 3, 2))
    return lax.conv_general_dilated(
        widened,
        flipped,
        (1, 1),
        ((1, 1), (0, 0)),
        dimension_numbers=("NHWC", "HWIO", "NHWC"),
        preferred_element_type=jnp.float32,
    )


def join_heads(stacked):
    return jnp.transpose(stacked, (1, 0, 2)).reshape(
        stacked.shape[1], stacked.shape[0] * stacked.shape[2]
    )


def head_math(q_head, k_head, v_head, g_head, blocks):
    softmax_scale = DH ** (-0.5)
    scores = (
        lax.dot_general(
            q_head, k_head, (((1,), (1,)), ((), ())), preferred_element_type=jnp.float32
        )
        * softmax_scale
    )
    top = jnp.max(scores, axis=1, keepdims=True)
    weights = jnp.exp(scores - top)
    probs = weights / jnp.sum(weights, axis=1, keepdims=True)
    probs_low = probs.astype(jnp.bfloat16)
    head_out = jnp.dot(probs_low, v_head, preferred_element_type=jnp.float32).astype(jnp.bfloat16)
    row_dot = jnp.sum(
        g_head.astype(jnp.float32) * head_out.astype(jnp.float32), axis=1, keepdims=True
    )
    prob_grad = lax.dot_general(
        g_head, v_head, (((1,), (1,)), ((), ())), preferred_element_type=jnp.float32
    )
    score_grad = (probs * (prob_grad - row_dot)).astype(jnp.bfloat16)
    q_grad = (
        jnp.dot(score_grad, k_head, preferred_element_type=jnp.float32) * softmax_scale
    ).astype(jnp.bfloat16)
    rows = q_head.shape[0] // blocks
    keys_total = k_head.shape[0]
    logit_tiles = score_grad.reshape(blocks, rows, keys_total)
    query_tiles = q_head.reshape(blocks, rows, q_head.shape[1])
    probability_tiles = probs_low.reshape(blocks, rows, keys_total)
    gradient_tiles = g_head.reshape(blocks, rows, g_head.shape[1])
    key_blocks = (
        lax.dot_general(
            logit_tiles,
            query_tiles,
            (((1,), (1,)), ((0,), (0,))),
            preferred_element_type=jnp.float32,
        )
        * softmax_scale
    ).astype(jnp.bfloat16)
    value_blocks = lax.dot_general(
        probability_tiles,
        gradient_tiles,
        (((1,), (1,)), ((0,), (0,))),
        preferred_element_type=jnp.float32,
    ).astype(jnp.bfloat16)
    key_portion = jnp.sum(key_blocks.astype(jnp.float32), axis=0).astype(jnp.bfloat16)
    value_portion = jnp.sum(value_blocks.astype(jnp.float32), axis=0).astype(jnp.bfloat16)
    return (q_grad, key_portion, value_portion)


def per_device(
    pre_activation,
    output_grad,
    up_kernel,
    in_kernel,
    final_weight,
    gate_table,
    bucket,
    query_vectors,
    key_vectors,
    value_vectors,
    out_weight,
    block_input,
):
    act_grad = column_grad(output_grad, up_kernel)
    feat_grad = (act_grad * silu_slope(pre_activation.astype(jnp.float32))).astype(jnp.bfloat16)
    latent_grad = column_grad(feat_grad, in_kernel).astype(jnp.bfloat16)
    row_group = lax.all_to_all(latent_grad, "seq", split_axis=1, concat_axis=2, tiled=True)
    tokens = query_vectors.shape[1]
    patch_rows = row_group.shape[1] // 2
    patch_cols = row_group.shape[2] // 2
    channels = row_group.shape[3]
    patches = (
        row_group.reshape(patch_rows, 2, patch_cols, 2, channels)
        .transpose(0, 2, 1, 3, 4)
        .reshape(tokens, 4 * channels)
    )
    stream_grad = jnp.dot(patches, final_weight, preferred_element_type=jnp.float32)
    picker = (jnp.arange(gate_table.shape[0], dtype=jnp.int32) == bucket[0]).astype(jnp.float32)
    gate_row = jnp.dot(picker, gate_table.astype(jnp.float32), precision=lax.Precision.HIGHEST)
    branch_grad = (stream_grad * gate_row[None, :]).astype(jnp.bfloat16)
    attn_grad = lax.dot_general(
        branch_grad, out_weight, (((1,), (1,)), ((), ())), preferred_element_type=jnp.float32
    ).astype(jnp.bfloat16)
    local_queries = query_vectors[0]
    local_input = block_input[0]
    width = local_queries.shape[1]
    seq_count = lax.axis_size("seq")
    group = width // seq_count
    head_count = group // DH

    def to_heads(values):
        return values.reshape(tokens, seq_count, group)

    q_in, k_in, v_in, g_in = (
        lax.all_to_all(to_heads(local_queries), "seq", split_axis=1, concat_axis=0, tiled=True),
        lax.all_to_all(to_heads(key_vectors[0]), "seq", split_axis=1, concat_axis=0, tiled=True),
        lax.all_to_all(to_heads(value_vectors[0]), "seq", split_axis=1, concat_axis=0, tiled=True),
        lax.all_to_all(to_heads(attn_grad), "seq", split_axis=1, concat_axis=0, tiled=True),
    )
    full = tokens * seq_count
    q_in = q_in.reshape(full, group)
    k_in = k_in.reshape(full, group)
    v_in = v_in.reshape(full, group)
    g_in = g_in.reshape(full, group)

    def group_head(head):
        start = head * DH
        return head_math(
            lax.dynamic_slice_in_dim(q_in, start, DH, 1),
            lax.dynamic_slice_in_dim(k_in, start, DH, 1),
            lax.dynamic_slice_in_dim(v_in, start, DH, 1),
            lax.dynamic_slice_in_dim(g_in, start, DH, 1),
            seq_count,
        )

    q_all, k_all, v_all = lax.map(group_head, jnp.arange(head_count, dtype=jnp.int32))

    def to_tokens_back(stacked):
        return join_heads(stacked).reshape(full, 1, group)

    q_back, k_back, v_back = (
        lax.all_to_all(to_tokens_back(q_all), "seq", split_axis=0, concat_axis=1, tiled=True),
        lax.all_to_all(to_tokens_back(k_all), "seq", split_axis=0, concat_axis=1, tiled=True),
        lax.all_to_all(to_tokens_back(v_all), "seq", split_axis=0, concat_axis=1, tiled=True),
    )
    query_grad = q_back.reshape(tokens, width)
    key_grad = k_back.reshape(tokens, width)
    value_grad = v_back.reshape(tokens, width)
    weight_grad = lax.psum_scatter(
        lax.dot_general(
            local_input, value_grad, (((0,), (0,)), ((), ())), preferred_element_type=jnp.float32
        ),
        ("dp", "seq"),
        scatter_dimension=0,
        tiled=True,
    )
    return (query_grad[None], key_grad[None], value_grad[None], weight_grad)


def solution(mesh):
    return jax.shard_map(
        per_device,
        mesh=mesh,
        in_specs=(
            P("dp", None, "seq", None),
            P("dp", None, "seq", None),
            P(),
            P(),
            P(),
            P(),
            P("dp"),
            P("dp", "seq", None),
            P("dp", "seq", None),
            P("dp", "seq", None),
            P(),
            P("dp", "seq", None),
        ),
        out_specs=(
            P("dp", "seq", None),
            P("dp", "seq", None),
            P("dp", "seq", None),
            P(("dp", "seq"), None),
        ),
        check_vma=False,
    )
```

profile of v0, /device:TPU:0, one launch (start us, length us, event | category | flops | bytes accessed | tf_op | source)
XLA Modules:
  0.0 442.2 jit_solution(7605344846664728169)
XLA Ops:
  7.2 1.5 copy.87
  8.7 5.1 %collective-permute-start = (bf16[1,16,1,512]{3,1,2,0:T(8,128)(2,1)S(1)}, bf16[1,16,1,512]{3,1,2,0:T(8,128)(2,1)S(1)}, u32[]{:S(2)}, u32[]{:S(2)}) collective-permute-start(bf16[1,16,1,512]{3,1,2,0:T(8,128)(2,1)S(1)} %get-tuple-element.195), channel_id=1, source_target_pairs={{0,1},{1,2},{2,3},{4,5},{5,6},{6,7},{8,9},{9,10},{10,11},{12,13},{... | collective-permute-start | bytes 49160 | tf_op jit(solution)/shard_map/ppermute | solution.py:14
  13.8 1.3 collective-permute-start.1
  15.2 4.2 collective-permute-done.1
  20.0 3.3 convolution_select_fusion
  24.9 3.5 collective-permute-start.2
  28.4 1.4 collective-permute-start.3
  29.9 4.3 collective-permute-done.3
  34.8 1.7 fusion.24
  37.4 3.3 all-to-all-start.2
  42.0 4.3 all-to-all-done.2
  46.3 3.5 all-to-all-start
  51.0 9.4 %all-to-all-done = bf16[128,4,512]{2,0,1:T(8,128)(2,1)S(1)} async-done(((bf16[128,4,512]{2,0,1:T(8,128)(2,1)}), bf16[128,4,512]{2,0,1:T(8,128)(2,1)S(1)}, u32[]{:S(2)}, u32[]{:S(2)}) %all-to-all-start) | async-done | bytes 524320 | tf_op jit(solution)/shard_map/all_to_all | solution.py:140
  60.5 3.5 all-to-all-start.1
  65.9 8.3 %all-to-all-done.1 = bf16[128,4,512]{2,0,1:T(8,128)(2,1)S(1)} async-done(((bf16[128,4,512]{2,0,1:T(8,128)(2,1)}), bf16[128,4,512]{2,0,1:T(8,128)(2,1)S(1)}, u32[]{:S(2)}, u32[]{:S(2)}) %all-to-all-start.1) | async-done | bytes 524320 | tf_op jit(solution)/shard_map/all_to_all | solution.py:141
  74.2 4.3 all-to-all-start.4
  79.1 9.1 %convolution_convert_fusion.2 = bf16[128,2048]{1,0:T(8,128)(2,1)S(1)} fusion(bf16[2048,3072]{1,0:T(8,128)(2,1)} %param.24, bf16[128,64]{0,1:T(8,128)(2,1)S(1)} %reshape.78, bf16[64,3072]{1,0:T(8,128)(2,1)S(1)} %copy-done.8, f32[3072]{0:T(1024)S(1)} %bitcast.164), kind=kOutput, calls=%fused_computation.36 | convolution fusion | flops 1661992960 | bytes 13529088 | tf_op jit(solution)/shard_map/dot_general | solution.py:126
  89.1 4.9 %all-to-all-start.3 = ((bf16[128,4,512]{2,0,1:T(8,128)(2,1)}), bf16[128,4,512]{2,0,1:T(8,128)(2,1)}, u32[]{:S(2)}, u32[]{:S(2)}) async-start(bf16[128,4,512]{2,0,1:T(8,128)(2,1)} %bitcast.108), calls=%async_computation.3 | async-start | bytes 1048576 | tf_op jit(solution)/shard_map/all_to_all | solution.py:143
  94.0 10.4 %all-to-all-done.3 = bf16[128,4,512]{2,0,1:T(8,128)(2,1)} async-done(((bf16[128,4,512]{2,0,1:T(8,128)(2,1)}), bf16[128,4,512]{2,0,1:T(8,128)(2,1)}, u32[]{:S(2)}, u32[]{:S(2)}) %all-to-all-start.3) | async-done | bytes 524320 | tf_op jit(solution)/shard_map/all_to_all | solution.py:143
  104.4 34.6 %while.17 = (s32[]{:T(128)}, bf16[4,512,128]{1,2,0:T(8,128)(2,1)}, bf16[4,512,128]{1,2,0:T(8,128)(2,1)}, bf16[4,512,128]{1,2,0:T(8,128)(2,1)}, s32[4]{0:T(128)S(...) while((s32[]{:T(128)}, bf16[4,512,128]{1,2,0:T(8,128)(2,1)}, ...), condition=%wide.region_6.7_spmd, body=%wide.region_0.6_spmd.sunk | while | flops 407435776 | bytes 11292887 | solution.py:161
  105.6 0.9 constant_dynamic-slice_fusion.8
  107.7 1.2 fusion.104
  108.9 1.3 fusion.105
  114.3 0.9 constant_dynamic-slice_fusion.8
  116.3 1.2 fusion.104
  117.5 1.3 fusion.105
  122.9 0.9 constant_dynamic-slice_fusion.8
  125.0 1.2 fusion.104
  126.2 1.3 fusion.105
  133.6 1.2 fusion.104
  134.9 1.3 fusion.105
  139.5 2.0 reduce.12
  142.1 12.8 %all_to_all.120 = bf16[4,2,32768]{2,1,0:T(2,128)(2,1)S(1)} all-to-all(bf16[4,2,32768]{2,1,0:T(2,128)(2,1)S(1)} %reshape.117), channel_id=1, replica_groups=mesh['dp'=8,'seq'=4] {'seq'}, dimensions={0} | all-to-all | bytes 1048576 | tf_op jit(solution)/shard_map/all_to_all | solution.py:169
  155.8 10.2 %convolution_bitcast_fusion = f32[3072,2048]{0,1:T(8,128)} fusion(bf16[128,2048]{0,1:T(8,128)(2,1)S(1)} %bitcast.144, bf16[1,128,3072]{2,1,0:T(8,128)(2,1)S(1)} %copy-done), kind=kOutput, calls=%fused_computation.33 | convolution fusion | flops 1610612736 | bytes 26476544 | tf_op jit(solution)/shard_map/dot_general | solution.py:175
  166.0 24.8 %copy.119 = f32[3072,2048]{1,0:T(8,128)} copy(f32[3072,2048]{0,1:T(8,128)} %convolution_bitcast_fusion) | data formatting | bytes 50331648
  190.9 1.0 copy-done.5
  191.9 1.0 reduce.11
  193.1 1.2 reshape.115
  194.3 3.5 all-to-all-start.6
  197.8 1.0 reduce.10
  198.9 1.2 reshape.113
  200.1 12.4 %all-to-all-done.6 = bf16[4,2,32768]{2,1,0:T(2,128)(2,1)S(1)} async-done(((bf16[4,2,32768]{2,1,0:T(2,128)(2,1)}), bf16[4,2,32768]{2,1,0:T(2,128)(2,1)S(1)}, u32[]{:S(2)}, u32[]{:S(2)}) %all-to-all-start.6) | async-done | bytes 524320 | tf_op jit(solution)/shard_map/all_to_all | solution.py:168
  212.5 3.5 all-to-all-start.5
  216.1 1.0 copy.115
  218.0 1.0 copy.114
  219.0 7.3 %all-to-all-done.5 = bf16[4,2,32768]{2,1,0:T(2,128)(2,1)S(1)} async-done(((bf16[4,2,32768]{2,1,0:T(2,128)(2,1)}), bf16[4,2,32768]{2,1,0:T(2,128)(2,1)S(1)}, u32[]{:S(2)}, u32[]{:S(2)}) %all-to-all-start.5) | async-done | bytes 524320 | tf_op jit(solution)/shard_map/all_to_all | solution.py:167
  227.3 1.0 copy.113
  228.3 207.1 %reduce-scatter.4.cloned.1.call-done = f32[96,2048]{1,0:T(8,128)} async-done(((f32[3072,2048]{1,0:T(8,128)}), f32[96,2048]{1,0:T(8,128)}) %reduce-scatter.4.cloned.1.call-update) | async-done | bytes 786448
  (133 shorter events, 31.9 us)
Async XLA Ops:
  7.2 148.7 %copy-start = (bf16[1,128,3072]{2,1,0:T(8,128)(2,1)S(1)}, bf16[1,128,3072]{2,1,0:T(8,128)(2,1)}, u32[]{:S(2)}) copy-start(bf16[1,128,3072]{2,1,0:T(8,128)(2,1)} %param.25) | copy-start | bytes 2359300
  7.2 12.8 %copy-start.10 = (bf16[3,3,512,512]{3,2,1,0:T(8,128)(2,1)S(1)}, bf16[3,3,512,512]{3,2,1,0:T(8,128)(2,1)}, u32[]{:S(2)}) copy-start(bf16[3,3,512,512]{3,2,1,0:T(8,128)(2,1)} %param.16) | copy-start | bytes 14155780
  8.7 6.5 %collective-permute-start = (bf16[1,16,1,512]{3,1,2,0:T(8,128)(2,1)S(1)}, bf16[1,16,1,512]{3,1,2,0:T(8,128)(2,1)S(1)}, u32[]{:S(2)}, u32[]{:S(2)}) collective-permute-start(bf16[1,16,1,512]{3,1,2,0:T(8,128)(2,1)S(1)} %get-tuple-element.195), channel_id=1, source_target_pairs={{0,1},{1,2},{2,3},{4,5},{5,6},{6,7},{8,9},{9,10},{10,11},{12,13},{... | collective-permute-start | bytes 49160 | tf_op jit(solution)/shard_map/ppermute | solution.py:14
  13.8 6.2 %copy-start.12 = (pred[8,5]{0,1:T(8,128)(4,1)S(1)}, pred[8,5]{0,1:T(8,128)(4,1)}, u32[]{:S(2)}) copy-start(pred[8,5]{0,1:T(8,128)(4,1)} %constant.80) | copy-start | bytes 124
  13.8 5.6 %collective-permute-start.1 = (bf16[1,16,1,512]{3,1,2,0:T(8,128)(2,1)S(1)}, bf16[1,16,1,512]{3,1,2,0:T(8,128)(2,1)S(1)}, u32[]{:S(2)}, u32[]{:S(2)}) collective-permute-start(bf16[1,16,1,512]{3,1,2,0:T(8,128)(2,1)S(1)} %get-tuple-element.196), channel_id=1, source_target_pairs={{1,0},{2,1},{3,2},{5,4},{6,5},{7,6},{9,8},{10,9},{11,10},{13,12},{... | collective-permute-start | bytes 49160 | tf_op jit(solution)/shard_map/ppermute | solution.py:17
  23.3 1.0 copy-start.7
  24.9 4.9 %collective-permute-start.2 = (bf16[1,16,1,512]{3,1,2,0:T(8,128)(2,1)S(1)}, bf16[1,16,1,512]{3,1,2,0:T(8,128)(2,1)S(1)}, u32[]{:S(2)}, u32[]{:S(2)}) collective-permute-start(bf16[1,16,1,512]{3,1,2,0:T(8,128)(2,1)S(1)} %get-tuple-element.193), channel_id=1, source_target_pairs={{0,1},{1,2},{2,3},{4,5},{5,6},{6,7},{8,9},{9,10},{10,11},{12,13},{... | collective-permute-start | bytes 49160 | tf_op jit(solution)/shard_map/ppermute | solution.py:14
  28.4 6.4 %copy-start.11 = (bf16[3,3,16,512]{3,2,1,0:T(8,128)(2,1)S(1)}, bf16[3,3,16,512]{3,2,1,0:T(8,128)(2,1)}, u32[]{:S(2)}) copy-start(bf16[3,3,16,512]{3,2,1,0:T(8,128)(2,1)} %param.17) | copy-start | bytes 442372
  28.4 5.8 %collective-permute-start.3 = (bf16[1,16,1,512]{3,1,2,0:T(8,128)(2,1)S(1)}, bf16[1,16,1,512]{3,1,2,0:T(8,128)(2,1)S(1)}, u32[]{:S(2)}, u32[]{:S(2)}) collective-permute-start(bf16[1,16,1,512]{3,1,2,0:T(8,128)(2,1)S(1)} %get-tuple-element.194), channel_id=1, source_target_pairs={{1,0},{2,1},{3,2},{5,4},{6,5},{7,6},{9,8},{10,9},{11,10},{13,12},{... | collective-permute-start | bytes 49160 | tf_op jit(solution)/shard_map/ppermute | solution.py:17
  34.8 5.9 %copy-start.2 = (bf16[1,128,2048]{2,1,0:T(8,128)(2,1)S(1)}, bf16[1,128,2048]{2,1,0:T(8,128)(2,1)}, u32[]{:S(2)}) copy-start(bf16[1,128,2048]{2,1,0:T(8,128)(2,1)} %param.21) | copy-start | bytes 1572868
  36.5 13.3 %copy-start.3 = (bf16[1,128,2048]{2,1,0:T(8,128)(2,1)S(1)}, bf16[1,128,2048]{2,1,0:T(8,128)(2,1)}, u32[]{:S(2)}) copy-start(bf16[1,128,2048]{2,1,0:T(8,128)(2,1)} %param.22) | copy-start | bytes 1572868
  37.4 8.8 %all-to-all-start.2 = ((bf16[4,2,1024]{2,1,0:T(2,128)(2,1)}), bf16[4,2,1024]{2,1,0:T(2,128)(2,1)S(1)}, u32[]{:S(2)}, u32[]{:S(2)}) async-start(bf16[4,2,1024]{2,1,0:T(2,128)(2,1)} %reshape.111), calls=%async_computation.2 | async-start | bytes 32768 | tf_op jit(solution)/shard_map/all_to_all | solution.py:112
  46.3 14.2 %all-to-all-start = ((bf16[128,4,512]{2,0,1:T(8,128)(2,1)}), bf16[128,4,512]{2,0,1:T(8,128)(2,1)S(1)}, u32[]{:S(2)}, u32[]{:S(2)}) async-start(bf16[128,4,512]{2,0,1:T(8,128)(2,1)} %copy.85), calls=%async_computation | async-start | bytes 1048576 | tf_op jit(solution)/shard_map/all_to_all | solution.py:140
  49.8 14.9 %copy-start.4 = (bf16[1,128,2048]{2,1,0:T(8,128)(2,1)S(1)}, bf16[1,128,2048]{2,1,0:T(8,128)(2,1)}, u32[]{:S(2)}) copy-start(bf16[1,128,2048]{2,1,0:T(8,128)(2,1)} %param.23) | copy-start | bytes 1572868
  60.5 13.7 %all-to-all-start.1 = ((bf16[128,4,512]{2,0,1:T(8,128)(2,1)}), bf16[128,4,512]{2,0,1:T(8,128)(2,1)S(1)}, u32[]{:S(2)}, u32[]{:S(2)}) async-start(bf16[128,4,512]{2,0,1:T(8,128)(2,1)} %copy.86), calls=%async_computation.1 | async-start | bytes 1048576 | tf_op jit(solution)/shard_map/all_to_all | solution.py:141
  63.9 14.6 %copy-start.9 = (bf16[8,3072]{1,0:T(8,128)(2,1)S(1)}, bf16[8,3072]{1,0:T(8,128)(2,1)}, u32[]{:S(2)}) copy-start(bf16[8,3072]{1,0:T(8,128)(2,1)} %param.19) | copy-start | bytes 147460
  64.6 14.5 %copy-start.8 = (bf16[64,3072]{1,0:T(8,128)(2,1)S(1)}, bf16[64,3072]{1,0:T(8,128)(2,1)}, u32[]{:S(2)}) copy-start(bf16[64,3072]{1,0:T(8,128)(2,1)} %param.18) | copy-start | bytes 1179652
  74.2 14.9 %all-to-all-start.4 = ((bf16[128,4,512]{2,0,1:T(8,128)(2,1)}), bf16[128,4,512]{2,0,1:T(8,128)(2,1)}, u32[]{:S(2)}, u32[]{:S(2)}) async-start(bf16[128,4,512]{2,0,1:T(8,128)(2,1)} %copy.101), calls=%async_computation.4 | async-start | bytes 1048576 | tf_op jit(solution)/shard_map/all_to_all | solution.py:142
  89.1 15.3 %all-to-all-start.3 = ((bf16[128,4,512]{2,0,1:T(8,128)(2,1)}), bf16[128,4,512]{2,0,1:T(8,128)(2,1)}, u32[]{:S(2)}, u32[]{:S(2)}) async-start(bf16[128,4,512]{2,0,1:T(8,128)(2,1)} %bitcast.108), calls=%async_computation.3 | async-start | bytes 1048576 | tf_op jit(solution)/shard_map/all_to_all | solution.py:143
  94.0 341.4 %reduce-scatter.4.cloned.1.call-start = ((), (), s32[]{:S(2)}) async-start(), calls=%async_computation.9 | async-start | bytes 25952256
  190.9 1.0 copy-start.5
  192.9 4.9 %copy-start.6 = (bf16[4,512,128]{1,2,0:T(8,128)(2,1)S(1)}, bf16[4,512,128]{1,2,0:T(8,128)(2,1)}, u32[]{:S(2)}) copy-start(bf16[4,512,128]{1,2,0:T(8,128)(2,1)} %get-tuple-element.143) | copy-start | bytes 1572868
  194.3 18.3 %all-to-all-start.6 = ((bf16[4,2,32768]{2,1,0:T(2,128)(2,1)}), bf16[4,2,32768]{2,1,0:T(2,128)(2,1)S(1)}, u32[]{:S(2)}, u32[]{:S(2)}) async-start(bf16[4,2,32768]{2,1,0:T(2,128)(2,1)} %reshape.115), calls=%async_computation.6 | async-start | bytes 1048576 | tf_op jit(solution)/shard_map/all_to_all | solution.py:168
  212.5 13.8 %all-to-all-start.5 = ((bf16[4,2,32768]{2,1,0:T(2,128)(2,1)}), bf16[4,2,32768]{2,1,0:T(2,128)(2,1)S(1)}, u32[]{:S(2)}, u32[]{:S(2)}) async-start(bf16[4,2,32768]{2,1,0:T(2,128)(2,1)} %reshape.113), calls=%async_computation.5 | async-start | bytes 1048576 | tf_op jit(solution)/shard_map/all_to_all | solution.py:167
  226.3 209.0 %copy-start.1 = (bf16[1,128,3072]{2,1,0:T(8,128)(2,1)S(1)}, bf16[1,128,3072]{2,1,0:T(8,128)(2,1)}, u32[]{:S(2)}) copy-start(bf16[1,128,3072]{2,1,0:T(8,128)(2,1)} %param.25) | copy-start | bytes 2359300
Sparse Core Ops, SparseCore 0:
  191.0 244.3 reduce-scatter.3
where the time goes:
time: 444 us; the launch traced here: 442 us
  waiting for transfers between devices  268 us (60%)
  local copies, waits for them, and re-layouts  58.5 us (13%)
  matrix products  40.3 us (9%)
  starting transfers between devices  37.7 us (8%)
  between operations  15.2 us (3%)
  blocking collectives  12.8 us (3%)
  other arithmetic  6.89 us (2%)
    unnamed x2, waiting for transfers between devices  207 us
    unnamed x45, local copies, waits for them, and re-layouts  36.8 us
    all_to_all x1, blocking collectives, per_device(): lax.all_to_all(to_tokens_back(v_all), 'seq', split_axis=0, concat_axis=1,...  12.8 us
    all_to_all x1, waiting for transfers between devices, per_device(): lax.all_to_all(to_tokens_back(k_all), 'seq', split_axis=0, concat_axis=1,...  12.4 us
    all_to_all x1, waiting for transfers between devices, per_device(): lax.all_to_all(to_heads(attn_grad), 'seq', split_axis=1, concat_axis=0, t...  10.4 us
    dot_general x1, matrix products, per_device(): lax.dot_general(local_input, value_grad, (((0,), (0,)), ((), ())), prefer...  10.2 us
    all_to_all x1, waiting for transfers between devices, per_device(): lax.all_to_all(to_heads(local_queries), 'seq', split_axis=1, concat_axis=...  9.43 us
    dot_general x1, matrix products, per_device(): lax.dot_general(branch_grad, out_weight, (((1,), (1,)), ((), ())), prefer...  9.11 us
  transfers between devices with their start and end apart: 12, of which 10 were waited for; matrix products, arithmetic and copies ran while one was open for 5% of the time, Pallas kernels for 0%

commit v1 on v0

v1 whole, which is shorter than its diff:
```python
import jax
import jax.numpy as jnp
from jax import lax
from jax.experimental import pallas as pl
from jax.experimental.pallas import tpu as pltpu
from jax.sharding import PartitionSpec as P

DH = 128


def silu_slope(values):
    sigma = jax.nn.sigmoid(values)
    return sigma * (1.0 + values * (1.0 - sigma))


def conv_grad(grad, kernel, rows_pad):
    flipped = jnp.transpose(kernel[::-1, ::-1], (0, 1, 3, 2))
    return lax.conv_general_dilated(
        grad,
        flipped,
        (1, 1),
        (rows_pad, (0, 0)),
        dimension_numbers=("NHWC", "HWIO", "NHWC"),
        preferred_element_type=jnp.float32,
    )


def head_kernel(q_ref, k_ref, v_ref, g_ref, qk_out, v_out):
    softmax_scale = DH ** (-0.5)
    blocks, _, rows, _ = q_ref.shape
    full = blocks * rows
    q_head = q_ref[:, 0].reshape(full, DH)
    k_head = k_ref[:, 0].reshape(full, DH)
    v_head = v_ref[:, 0].reshape(full, DH)
    g_head = g_ref[...]

    def rows_by_rows(a, b):
        return lax.dot_general(a, b, (((1,), (1,)), ((), ())), preferred_element_type=jnp.float32)

    def columns_by_columns(a, b):
        return lax.dot_general(a, b, (((0,), (0,)), ((), ())), preferred_element_type=jnp.float32)

    scores = rows_by_rows(q_head, k_head) * softmax_scale
    weights = jnp.exp(scores - jnp.max(scores, axis=1, keepdims=True))
    probs = weights * (1.0 / jnp.sum(weights, axis=1, keepdims=True))
    probs_low = probs.astype(jnp.bfloat16)
    head_out = jnp.dot(probs_low, v_head, preferred_element_type=jnp.float32).astype(jnp.bfloat16)
    row_dot = jnp.sum(
        g_head.astype(jnp.float32) * head_out.astype(jnp.float32), axis=1, keepdims=True
    )
    prob_grad = rows_by_rows(g_head, v_head)
    score_grad = (probs * (prob_grad - row_dot)).astype(jnp.bfloat16)
    q_grad = jnp.dot(score_grad, k_head, preferred_element_type=jnp.float32) * softmax_scale
    k_grad = columns_by_columns(score_grad, q_head) * softmax_scale
    v_grad = columns_by_columns(probs_low, g_head)
    qk_out[:, 0] = q_grad.astype(jnp.bfloat16).reshape(blocks, rows, DH)
    qk_out[:, 1] = k_grad.astype(jnp.bfloat16).reshape(blocks, rows, DH)
    v_out[...] = v_grad.astype(jnp.bfloat16).reshape(blocks, rows, DH)


def attention_backward(qkv, grad):
    blocks, _, rows, group = qkv.shape
    full = blocks * rows

    def part(which):
        return pl.BlockSpec((blocks, 1, rows, DH), lambda h: (0, which, 0, h))

    heads = group // DH
    return pl.pallas_call(
        head_kernel,
        grid=(heads,),
        in_specs=[part(0), part(1), part(2), pl.BlockSpec((full, DH), lambda h: (0, h))],
        out_specs=[
            pl.BlockSpec((blocks, 2, rows, DH), lambda h: (0, 0, 0, h)),
            pl.BlockSpec((blocks, rows, DH), lambda h: (0, 0, h)),
        ],
        out_shape=[
            jax.ShapeDtypeStruct((blocks, 2, rows, group), jnp.bfloat16),
            jax.ShapeDtypeStruct((blocks, rows, group), jnp.bfloat16),
        ],
        compiler_params=pltpu.CompilerParams(vmem_limit_bytes=48 * 2**20),
        cost_estimate=pl.CostEstimate(
            flops=14 * heads * full * full * DH,
            bytes_accessed=14 * full * group,
            transcendentals=heads * full * full,
        ),
    )(qkv, qkv, qkv, grad)


def per_device(
    pre_activation,
    output_grad,
    up_kernel,
    in_kernel,
    final_weight,
    gate_table,
    bucket,
    query_vectors,
    key_vectors,
    value_vectors,
    out_weight,
    block_input,
):
    seq_count = lax.axis_size("seq")
    dp_count = lax.axis_size("dp")
    seq_index = lax.axis_index("seq")
    tokens, width = query_vectors.shape[1:]
    group = width // seq_count
    full = tokens * seq_count
    model = block_input.shape[2]

    forward = [(i, i + 1) for i in range(seq_count - 1)]
    backward = [(target, source) for source, target in forward]
    low = lax.ppermute(
        jnp.concatenate([output_grad[:, :, -2:], pre_activation[:, :, -1:]], axis=2), "seq", forward
    )
    high = lax.ppermute(
        jnp.concatenate([output_grad[:, :, :2], pre_activation[:, :, :1]], axis=2), "seq", backward
    )
    qkv = jnp.stack([query_vectors[0], key_vectors[0], value_vectors[0]])
    qkv = qkv.reshape(3, tokens, seq_count, group).transpose(2, 0, 1, 3)
    qkv = lax.all_to_all(qkv, "seq", split_axis=0, concat_axis=0, tiled=True)
    rows_block = model // dp_count
    inputs = block_input[0].reshape(tokens, dp_count, rows_block).transpose(1, 0, 2)
    inputs = lax.all_to_all(inputs, "dp", split_axis=0, concat_axis=0, tiled=True)
    inputs = inputs.reshape(dp_count * tokens, rows_block)

    wide_grad = jnp.concatenate([low[:, :, :2], output_grad, high[:, :, :2]], axis=2)
    wide_pre = jnp.concatenate([low[:, :, 2:], pre_activation, high[:, :, 2:]], axis=2)
    act_grad = conv_grad(wide_grad, up_kernel, (1, 1))
    columns = jnp.arange(wide_pre.shape[2])
    inside = ((columns > 0) | (seq_index > 0)) & (
        (columns < wide_pre.shape[2] - 1) | (seq_index < seq_count - 1)
    )
    feat_grad = act_grad * silu_slope(wide_pre.astype(jnp.float32))
    feat_grad = jnp.where(inside[None, None, :, None], feat_grad, 0.0).astype(jnp.bfloat16)
    latent_grad = conv_grad(feat_grad, in_kernel, (1, 1)).astype(jnp.bfloat16)

    _, lat_rows, lat_cols, channels = latent_grad.shape
    patch_rows, patch_cols = lat_rows // 2, lat_cols // 2
    patches = (
        latent_grad.reshape(patch_rows, 2, patch_cols, 2, channels)
        .transpose(0, 2, 1, 3, 4)
        .reshape(1, patch_rows * patch_cols, 4 * channels)
    )
    patches = jnp.broadcast_to(patches, (seq_count,) + patches.shape[1:])
    patches = lax.all_to_all(patches, "seq", split_axis=0, concat_axis=0, tiled=True)
    patches = (
        patches.reshape(seq_count, patch_rows, patch_cols, 4 * channels)
        .transpose(1, 0, 2, 3)
        .reshape(full, 4 * channels)
    )
    stream_grad = jnp.dot(patches, final_weight, preferred_element_type=jnp.float32)
    gate_row = lax.dynamic_slice_in_dim(gate_table, bucket[0], 1, 0).astype(jnp.float32)
    branch_grad = (stream_grad * gate_row).astype(jnp.bfloat16)
    group_weight = lax.dynamic_slice_in_dim(out_weight, seq_index * group, group, 0)
    attn_grad = lax.dot_general(
        branch_grad, group_weight, (((1,), (1,)), ((), ())), preferred_element_type=jnp.float32
    ).astype(jnp.bfloat16)

    qk_grad, v_grad = attention_backward(qkv, attn_grad)
    v_grad = lax.all_to_all(v_grad, "seq", split_axis=0, concat_axis=0, tiled=True)
    value_grad = v_grad.transpose(1, 0, 2).reshape(tokens, width)
    values = lax.all_gather(value_grad, "dp", axis=0, tiled=True)
    qk_grad = lax.all_to_all(qk_grad, "seq", split_axis=0, concat_axis=0, tiled=True)
    qk_grad = qk_grad.transpose(1, 2, 0, 3).reshape(2, tokens, width)
    term = lax.dot_general(
        inputs, values, (((0,), (0,)), ((), ())), preferred_element_type=jnp.float32
    ).astype(jnp.bfloat16)
    terms = lax.all_to_all(
        term.reshape(seq_count, rows_block // seq_count, width),
        "seq", split_axis=0, concat_axis=0, tiled=True,
    )
    weight_grad = jnp.sum(terms.astype(jnp.float32), axis=0)
    return (qk_grad[:1], qk_grad[1:], value_grad[None], weight_grad)


def solution(mesh):
    return jax.shard_map(
        per_device,
        mesh=mesh,
        in_specs=(
            P("dp", None, "seq", None),
            P("dp", None, "seq", None),
            P(),
            P(),
            P(),
            P(),
            P("dp"),
            P("dp", "seq", None),
            P("dp", "seq", None),
            P("dp", "seq", None),
            P(),
            P("dp", "seq", None),
        ),
        out_specs=(
            P("dp", "seq", None),
            P("dp", "seq", None),
            P("dp", "seq", None),
            P(("dp", "seq"), None),
        ),
        check_vma=False,
    )
```

time: 444 us -> 210 us (0.47)
  waiting for transfers between devices: 268 us -> 81 us
  local copies, waits for them, and re-layouts: 58.5 us -> 20.1 us
  blocking collectives: 12.8 us -> 38.2 us
  matrix products: 40.3 us -> 19 us
  starting transfers between devices: 37.7 us -> 23.9 us
  Pallas kernels: 0 us -> 7.33 us
    unnamed x2 -> x1, waiting for transfers between devices: 207 us -> 0.02 us
    unnamed x45 -> x26, local copies, waits for them, and re-layouts: 36.8 us -> 8.26 us
    dot_general x27 -> x2, matrix products: 35.3 us -> 9.69 us  [the longest x1 5.21 us: per_device(): lax.dot_general(inputs, values, (((0,), (0,)), ((), ())), preferred_eleme...]
    all_to_all x1 -> x2, blocking collectives: 12.8 us -> 38.2 us  [the longest x1 21.7 us: per_device(): lax.all_to_all(inputs, 'dp', split_axis=0, concat_axis=0, tiled=True)]
    all_gather x0 -> x1, waiting for transfers between devices: none -> 14.6 us  [per_device(): values = lax.all_gather(value_grad, 'dp', axis=0, tiled=True)]
    all_to_all x7 -> x4, waiting for transfers between devices: 52.1 us -> 66.4 us  [the longest x1 30.6 us: per_device(): lax.all_to_all(term.reshape(seq_count, rows_block // seq_count, width), '...]
    all_to_all x7 -> x4, starting transfers between devices: 26.4 us -> 16.3 us  [the longest x1 5.43 us: per_device(): lax.all_to_all(patches, 'seq', split_axis=0, concat_axis=0, tiled=True)]
    ppermute x4 -> x2, waiting for transfers between devices: 8.66 us -> 0.01 us  [the longest x1 0.01 us: per_device(): lax.ppermute(jnp.concatenate([output_grad[:, :, :2], pre_activation[:, :,...]
  transfers between devices with their start and end apart: 12 -> 7, of which waited for: 10 -> 5; matrix products, arithmetic and copies ran while one was open for 5% -> 11% of each run, Pallas kernels for 0% -> 0%
where the time goes in v1:
time: 210 us; the launch traced here: 208 us
  waiting for transfers between devices  81 us (39%)
  blocking collectives  38.2 us (18%)
  starting transfers between devices  23.9 us (11%)
  local copies, waits for them, and re-layouts  20.1 us (10%)
  matrix products  19 us (9%)
  between operations  15 us (7%)
  Pallas kernels  7.33 us (3%)
  other arithmetic  3.92 us (2%)
    all_to_all x1, waiting for transfers between devices, per_device(): lax.all_to_all(term.reshape(seq_count, rows_block // seq_count, width), '...  30.6 us
    all_to_all x1, waiting for transfers between devices, per_device(): qkv = lax.all_to_all(qkv, 'seq', split_axis=0, concat_axis=0, tiled=True)  27.2 us
    all_to_all x1, blocking collectives, per_device(): lax.all_to_all(inputs, 'dp', split_axis=0, concat_axis=0, tiled=True)  21.7 us
    all_to_all x1, blocking collectives, per_device(): lax.all_to_all(v_grad, 'seq', split_axis=0, concat_axis=0, tiled=True)  16.5 us
    all_gather x1, waiting for transfers between devices, per_device(): values = lax.all_gather(value_grad, 'dp', axis=0, tiled=True)  14.6 us
    conv_general_dilated x2, matrix products, conv_grad(): lax.conv_general_dilated(grad, flipped, (1, 1), (rows_pad, (0, 0)), dimen...  9.29 us
    unnamed x26, local copies, waits for them, and re-layouts  8.26 us
    pallas_call x1, Pallas kernels, attention_backward(): pl.pallas_call(head_kernel, grid=(heads,), in_specs=[part(0), part(1), pa...  7.33 us
  transfers between devices with their start and end apart: 7, of which 5 were waited for; matrix products, arithmetic and copies ran while one was open for 11% of the time, Pallas kernels for 0%

profile of v1, /device:TPU:0, one launch (start us, length us, event | category | flops | bytes accessed | tf_op | source)
XLA Modules:
  0.0 208.4 jit_solution(13847130147212140279)
XLA Ops:
  7.2 1.4 copy.71
  8.7 1.3 copy.70
  10.0 0.6 pad_maximum_fusion.2
  10.6 1.3 collective-permute-start.1
  11.9 0.6 pad_maximum_fusion.1
  12.6 6.2 %collective-permute-start = (bf16[1,16,3,512]{3,1,2,0:T(8,128)(2,1)}, bf16[1,16,3,512]{3,1,2,0:T(8,128)(2,1)}, u32[]{:S(2)}, u32[]{:S(2)}) collective-permute-start(bf16[1,16,3,512]{3,1,2,0:T(8,128)(2,1)} %pad_maximum_fusion.1), channel_id=1, source_target_pairs={{0,1},{1,2},{2,3},{4,5},{5,6},{6,7},{8,9},{9,10},{10,11},{12,13},{... | collective-permute-start | bytes 147464 | tf_op jit(solution)/shard_map/ppermute | solution.py:114
  18.7 0.3 copy.66
  19.0 0.3 copy.67
  19.3 1.3 copy.68
  20.6 0.8 slice.55
  21.4 0.8 slice.52
  22.3 0.4 copy.76
  22.9 5.3 %convolution_select_fusion = f32[16,8,5,512]{3,1,2,0:T(8,128)S(1)} fusion(bf16[3,3,512,512]{3,2,1,0:T(8,128)(2,1)} %param.14, bf16[16,1,7,2,512]{4,2,3,0,1:T(8,128)(2,1)S(1)} %slice.56, bf16[16,1,8,5,512]{4,2,3,0,1:T(8,128)(2,1)S(1)} %copy.76, pred[8,5]{0,1:T(8,128)(4,1)S(1)} %copy-done.7), kind=kOutput, calls=%fused_computation.10 | convolution fusion | flops 2897149952 | bytes 6914088 | tf_op jit(solution)/shard_map/conv_general_dilated | solution.py:18
  28.2 0.8 copy.77
  29.0 0.8 slice.59
  29.7 0.7 slice.58
  30.5 0.5 fusion.13
  30.9 4.0 %convolution_convert_fusion.1 = bf16[1,16,32,16]{3,0,2,1:T(2,128)(2,1)S(1)} fusion(bf16[3,3,16,512]{3,2,1,0:T(8,128)(2,1)S(1)} %copy-done.6, bf16[1,16,34,512]{3,1,2,0:T(8,128)(2,1)S(1)} %fusion.13), kind=kOutput, calls=%fused_computation.12 | convolution fusion | flops 72359936 | bytes 720896 | tf_op jit(solution)/shard_map/conv_general_dilated | solution.py:18
  35.3 0.6 broadcast_in_dim.23
  35.9 5.4 %all-to-all-start.1 = ((bf16[4,128,64]{1,2,0:T(8,128)(2,1)}), bf16[4,128,64]{1,2,0:T(8,128)(2,1)}, u32[]{:S(2)}, u32[]{:S(2)}) async-start(bf16[4,128,64]{1,2,0:T(8,128)(2,1)} %broadcast_in_dim.23), calls=%async_computation.1 | async-start | bytes 131072 | tf_op jit(solution)/shard_map/all_to_all | solution.py:147
  41.3 0.2 pad_maximum_fusion
  41.5 1.6 copy.69
  43.1 4.1 %all-to-all-done.1 = bf16[4,128,64]{1,2,0:T(8,128)(2,1)} async-done(((bf16[4,128,64]{1,2,0:T(8,128)(2,1)}), bf16[4,128,64]{1,2,0:T(8,128)(2,1)}, u32[]{:S(2)}, u32[]{:S(2)}) %all-to-all-start.1) | async-done | bytes 65568 | tf_op jit(solution)/shard_map/all_to_all | solution.py:147
  47.2 3.6 %all-to-all-start = ((bf16[4,3,128,512]{3,2,1,0:T(8,128)(2,1)}), bf16[4,3,128,512]{3,2,1,0:T(8,128)(2,1)S(1)}, u32[]{:S(2)}, u32[]{:S(2)}) async-start(bf16[4,3,128,512]{3,2,1,0:T(8,128)(2,1)} %bitcast.1), calls=%async_computation | async-start | bytes 3145728 | tf_op jit(solution)/shard_map/all_to_all | solution.py:122
  50.8 0.2 all-gather.2.cloned.1.call-start
  51.6 0.8 dynamic-slice_convert_fusion
  52.5 1.0 copy.81
  53.5 4.5 %fusion.3.g_ref = bf16[512,512]{1,0:T(8,128)(2,1)S(1)} fusion(bf16[2048,3072]{1,0:T(8,128)(2,1)} %param.22, s32[]{:T(128)S(6)} %select_n.12, bf16[512,64]{1,0:T(8,128)(2,1)S(1)} %bitcast.62, bf16[64,3072]{1,0:T(8,128)(2,1)S(1)} %copy-done, f32[3072]{0:T(1024)S(1)} %bitcast.63), kind=kOutput, calls=%fused_computation.11 | convolution fusion | flops 1815347200 | bytes 4141060 | tf_op jit(solution)/shard_map/dot_general | solution.py:157
  57.9 27.2 %all-to-all-done.q_ref.k_ref.v_ref = bf16[4,3,128,512]{3,2,1,0:T(8,128)(2,1)S(1)} async-done(((bf16[4,3,128,512]{3,2,1,0:T(8,128)(2,1)}), bf16[4,3,128,512]{3,2,1,0:T(8,128)(2,1)S(1)}, u32[]{:S(2)}, u32[]{:S(2)}) %all-to-all-start) | async-done | bytes 1572896 | tf_op jit(solution)/shard_map/all_to_all | solution.py:122
  85.1 7.3 %shard_map.147 = (bf16[4,2,128,512]{3,2,1,0:T(8,128)(2,1)}, bf16[4,128,512]{2,1,0:T(8,128)(2,1)S(1)}) custom-call(bf16[4,3,128,512]{3,2,1,0:T(8,128)(2,1)S(1)} %all-to-all-done.q_ref.k_ref.v_ref, bf16[4,3,128,512]{3,2,1,0:T(8,128)(2,1)S(1)} %all-to-all-done.q_ref.k_ref.v_ref, bf16[4,3,128,512]{3,2,1,0:T(8,128)(2,1)S(1)} %all-to-all-done.q_ref.k_ref.v_ref, ...), custom_call_target="tpu_custom_call" | custom-call | flops 1879048192 | bytes 3670016 | tf_op jit(solution)/shard_map/pallas_call | solution.py:69
  92.5 16.5 %all_to_all.30 = bf16[4,128,512]{2,1,0:T(8,128)(2,1)S(1)} all-to-all(bf16[4,128,512]{2,1,0:T(8,128)(2,1)S(1)} %get-tuple-element.7), channel_id=1, replica_groups=mesh['dp'=8,'seq'=4] {'seq'}, dimensions={0} | all-to-all | bytes 1048576 | tf_op jit(solution)/shard_map/all_to_all | solution.py:162
  108.9 1.0 copy.85
  110.0 0.4 copy.87
  110.4 21.7 %all_to_all.31 = bf16[8,128,384]{1,2,0:T(8,128)(2,1)S(1)} all-to-all(bf16[8,128,384]{1,2,0:T(8,128)(2,1)S(1)} %bitcast.53), channel_id=1, replica_groups=mesh['dp'=8,'seq'=4] {'dp'}, dimensions={0} | all-to-all | bytes 1572864 | tf_op jit(solution)/shard_map/all_to_all | solution.py:125
  132.0 3.6 %all-to-all-start.2 = ((bf16[4,2,128,512]{3,2,1,0:T(8,128)(2,1)}), bf16[4,2,128,512]{3,2,1,0:T(8,128)(2,1)S(1)}, u32[]{:S(2)}, u32[]{:S(2)}) async-start(bf16[4,2,128,512]{3,2,1,0:T(8,128)(2,1)} %get-tuple-element.6), calls=%async_computation.2 | async-start | bytes 2097152 | tf_op jit(solution)/shard_map/all_to_all | solution.py:165
  135.6 0.4 copy.88
  136.0 14.6 %all-gather.2.cloned.1.call-done = bf16[1024,2048]{0,1:T(8,128)(2,1)} async-done(((bf16[128,2048]{0,1:T(8,128)(2,1)}), bf16[1024,2048]{0,1:T(8,128)(2,1)}) %all-gather.2.cloned.1.call-update) | async-done | bytes 4194320 | tf_op jit(solution)/shard_map/all_gather | solution.py:164
  150.6 5.2 %convolution_convert_fusion = bf16[2048,384]{0,1:T(8,128)(2,1)} fusion(bf16[1024,2048]{0,1:T(8,128)(2,1)} %all-gather.2.cloned.1.call-done, bf16[1024,384]{1,0:T(8,128)(2,1)S(1)} %bitcast.59), kind=kOutput, calls=%fused_computation.4 | convolution fusion | flops 1611399168 | bytes 6553600 | tf_op jit(solution)/shard_map/dot_general | solution.py:167
  155.8 4.5 %all-to-all-done.2 = bf16[4,2,128,512]{3,2,1,0:T(8,128)(2,1)S(1)} async-done(((bf16[4,2,128,512]{3,2,1,0:T(8,128)(2,1)}), bf16[4,2,128,512]{3,2,1,0:T(8,128)(2,1)S(1)}, u32[]{:S(2)}, u32[]{:S(2)}) %all-to-all-start.2) | async-done | bytes 1048608 | tf_op jit(solution)/shard_map/all_to_all | solution.py:165
  160.3 3.7 %all-to-all-start.5 = ((bf16[4,96,2048]{2,1,0:T(8,128)(2,1)}), bf16[4,96,2048]{2,1,0:T(8,128)(2,1)S(1)}, u32[]{:S(2)}, u32[]{:S(2)}) async-start(bf16[4,96,2048]{2,1,0:T(8,128)(2,1)} %bitcast.58), calls=%async_computation.5 | async-start | bytes 3145728 | tf_op jit(solution)/shard_map/all_to_all | solution.py:170
  164.0 1.0 copy.91
  165.0 1.1 fusion.26
  166.1 1.4 copy.84
  167.5 1.0 copy.90
  168.5 0.3 copy.83
  168.8 1.0 copy.89
  169.8 30.6 %all-to-all-done.5 = bf16[4,96,2048]{2,1,0:T(8,128)(2,1)S(1)} async-done(((bf16[4,96,2048]{2,1,0:T(8,128)(2,1)}), bf16[4,96,2048]{2,1,0:T(8,128)(2,1)S(1)}, u32[]{:S(2)}, u32[]{:S(2)}) %all-to-all-start.5) | async-done | bytes 1572896 | tf_op jit(solution)/shard_map/all_to_all | solution.py:170
  200.4 1.1 convert_reduce_fusion
  (29 shorter events, 0.8 us)
Async XLA Ops:
  7.2 46.3 %copy-start = (bf16[64,3072]{1,0:T(8,128)(2,1)S(1)}, bf16[64,3072]{1,0:T(8,128)(2,1)}, u32[]{:S(2)}) copy-start(bf16[64,3072]{1,0:T(8,128)(2,1)} %param.16) | copy-start | bytes 1179652
  7.2 11.5 %copy-start.4 = (bf16[1,128,2048]{2,1,0:T(8,128)(2,1)S(1)}, bf16[1,128,2048]{2,1,0:T(8,128)(2,1)}, u32[]{:S(2)}) copy-start(bf16[1,128,2048]{2,1,0:T(8,128)(2,1)} %param.19) | copy-start | bytes 1572868
  7.2 11.8 %copy-start.5 = (bf16[1,128,2048]{2,1,0:T(8,128)(2,1)S(1)}, bf16[1,128,2048]{2,1,0:T(8,128)(2,1)}, u32[]{:S(2)}) copy-start(bf16[1,128,2048]{2,1,0:T(8,128)(2,1)} %param.20) | copy-start | bytes 1572868
  10.6 10.0 %collective-permute-start.1 = (bf16[1,16,3,512]{3,1,2,0:T(8,128)(2,1)}, bf16[1,16,3,512]{3,1,2,0:T(8,128)(2,1)}, u32[]{:S(2)}, u32[]{:S(2)}) collective-permute-start(bf16[1,16,3,512]{3,1,2,0:T(8,128)(2,1)} %pad_maximum_fusion.2), channel_id=1, source_target_pairs={{1,0},{2,1},{3,2},{5,4},{6,5},{7,6},{9,8},{10,9},{11,10},{13,12},{... | collective-permute-start | bytes 147464 | tf_op jit(solution)/shard_map/ppermute | solution.py:117
  12.6 8.8 %collective-permute-start = (bf16[1,16,3,512]{3,1,2,0:T(8,128)(2,1)}, bf16[1,16,3,512]{3,1,2,0:T(8,128)(2,1)}, u32[]{:S(2)}, u32[]{:S(2)}) collective-permute-start(bf16[1,16,3,512]{3,1,2,0:T(8,128)(2,1)} %pad_maximum_fusion.1), channel_id=1, source_target_pairs={{0,1},{1,2},{2,3},{4,5},{5,6},{6,7},{8,9},{9,10},{10,11},{12,13},{... | collective-permute-start | bytes 147464 | tf_op jit(solution)/shard_map/ppermute | solution.py:114
  22.2 0.7 copy-start.7
  29.0 1.9 copy-start.6
  35.9 11.3 %all-to-all-start.1 = ((bf16[4,128,64]{1,2,0:T(8,128)(2,1)}), bf16[4,128,64]{1,2,0:T(8,128)(2,1)}, u32[]{:S(2)}, u32[]{:S(2)}) async-start(bf16[4,128,64]{1,2,0:T(8,128)(2,1)} %broadcast_in_dim.23), calls=%async_computation.1 | async-start | bytes 131072 | tf_op jit(solution)/shard_map/all_to_all | solution.py:147
  47.2 37.9 %all-to-all-start = ((bf16[4,3,128,512]{3,2,1,0:T(8,128)(2,1)}), bf16[4,3,128,512]{3,2,1,0:T(8,128)(2,1)S(1)}, u32[]{:S(2)}, u32[]{:S(2)}) async-start(bf16[4,3,128,512]{3,2,1,0:T(8,128)(2,1)} %bitcast.1), calls=%async_computation | async-start | bytes 3145728 | tf_op jit(solution)/shard_map/all_to_all | solution.py:122
  50.8 99.9 %all-gather.2.cloned.1.call-start = ((), (), s32[]{:S(2)}) async-start(), calls=%async_computation.6 | async-start | bytes 4718592 | tf_op jit(solution)/shard_map/all_gather | solution.py:164
  92.5 17.5 %copy-start.3 = (bf16[1,128,3072]{2,1,0:T(8,128)(2,1)S(1)}, bf16[1,128,3072]{2,1,0:T(8,128)(2,1)}, u32[]{:S(2)}) copy-start(bf16[1,128,3072]{2,1,0:T(8,128)(2,1)} %param.23) | copy-start | bytes 2359300
  132.0 28.3 %all-to-all-start.2 = ((bf16[4,2,128,512]{3,2,1,0:T(8,128)(2,1)}), bf16[4,2,128,512]{3,2,1,0:T(8,128)(2,1)S(1)}, u32[]{:S(2)}, u32[]{:S(2)}) async-start(bf16[4,2,128,512]{3,2,1,0:T(8,128)(2,1)} %get-tuple-element.6), calls=%async_computation.2 | async-start | bytes 2097152 | tf_op jit(solution)/shard_map/all_to_all | solution.py:165
  160.3 3.7 %copy-start.1 = (bf16[128,4,512]{0,2,1:T(8,128)(2,1)S(1)}, bf16[128,4,512]{0,2,1:T(8,128)(2,1)}, u32[]{:S(2)}) copy-start(bf16[128,4,512]{0,2,1:T(8,128)(2,1)} %copy.85) | copy-start | bytes 1572868
  160.3 40.1 %all-to-all-start.5 = ((bf16[4,96,2048]{2,1,0:T(8,128)(2,1)}), bf16[4,96,2048]{2,1,0:T(8,128)(2,1)S(1)}, u32[]{:S(2)}, u32[]{:S(2)}) async-start(bf16[4,96,2048]{2,1,0:T(8,128)(2,1)} %bitcast.58), calls=%async_computation.5 | async-start | bytes 3145728 | tf_op jit(solution)/shard_map/all_to_all | solution.py:170
  166.1 2.4 %copy-start.2 = (bf16[1,128,4,512]{3,1,0,2:T(8,128)(2,1)S(1)}, bf16[1,128,4,512]{3,1,0,2:T(8,128)(2,1)}, u32[]{:S(2)}) copy-start(bf16[1,128,4,512]{3,1,0,2:T(8,128)(2,1)} %get-tuple-element.21) | copy-start | bytes 1572868
Sparse Core Ops, SparseCore 0:
  110.1 40.4 all-gather.1

commit v2 on v1

--- a/solution.py
+++ b/solution.py
@@ -1,3 +1,5 @@
+import functools
+
 import jax
 import jax.numpy as jnp
 from jax import lax
@@ -85,6 +87,174 @@
             transcendentals=heads * full * full,
         ),
     )(qkv, qkv, qkv, grad)
+
+
+def return_kernel(seq_count, dp_count, v_ref, qk_ref, x_ref, qk_out, v_out, w_out,
+                  own, gathered, terms, arrived, x_send, x_recv, v_send, v_recv,
+                  qk_send, qk_recv, g_send, g_recv, t_send, t_recv, here):
+    seq_index, dp_index = lax.axis_index("seq"), lax.axis_index("dp")
+    _, tokens, group = v_ref.shape
+
+    def seq_peer(step):
+        return lax.rem(seq_index + step, seq_count)
+
+    def dp_peer(step):
+        return lax.rem(dp_index + step, dp_count)
+
+    def columns(block):
+        return pl.ds(pl.multiple_of(block * group, group), group)
+
+    def slot(step):
+        return pl.ds(step * tokens, tokens)
+
+    def to_seq(source, target, send, recv, step):
+        return pltpu.make_async_remote_copy(
+            src_ref=source, dst_ref=target, send_sem=send, recv_sem=recv,
+            device_id={"seq": seq_peer(step)}, device_id_type=pl.DeviceIdType.MESH,
+        )
+
+    def to_dp(source, target, send, recv, step):
+        return pltpu.make_async_remote_copy(
+            src_ref=source, dst_ref=target, send_sem=send, recv_sem=recv,
+            device_id={"dp": dp_peer(step)}, device_id_type=pl.DeviceIdType.MESH,
+        )
+
+    barrier = pltpu.get_barrier_semaphore()
+    for step in range(1, seq_count):
+        pl.semaphore_signal(
+            barrier, inc=1, device_id={"seq": seq_peer(step)}, device_id_type=pl.DeviceIdType.MESH
+        )
+    for step in range(1, dp_count):
+        pl.semaphore_signal(
+            barrier, inc=1, device_id={"dp": dp_peer(step)}, device_id_type=pl.DeviceIdType.MESH
+        )
+    pl.semaphore_wait(barrier, seq_count + dp_count - 2)
+
+    v_copies = [
+        to_seq(v_ref.at[seq_peer(e)], gathered.at[e, slot(0)], v_send.at[e], v_recv.at[e], e)
+        for e in range(1, seq_count)
+    ]
+    for copy in v_copies:
+        copy.start()
+    x_copies = [
+        to_dp(x_ref.at[dp_peer(d)], own.at[slot(d)], x_send.at[d], x_recv.at[d], d)
+        for d in range(1, dp_count)
+    ]
+    for copy in x_copies:
+        copy.start()
+    gathered[0, slot(0)] = v_ref[seq_index]
+
+    def gather(c):
+        copies = [
+            to_dp(
+                gathered.at[c, slot(0)], gathered.at[c, slot(d)], g_send.at[c, d], g_recv.at[c, d], d
+            )
+            for d in range(1, dp_count)
+        ]
+        for copy in copies:
+            copy.start()
+        return copies
+
+    g_copies = [gather(0)]
+    qk_copies = [
+        to_seq(
+            qk_ref.at[seq_peer(e)], qk_out.at[:, :, columns(seq_index)],
+            qk_send.at[e], qk_recv.at[e], e,
+        )
+        for e in range(1, seq_count)
+    ]
+    for copy in qk_copies:
+        copy.start()
+    mine = pltpu.make_async_copy(
+        qk_ref.at[seq_index], qk_out.at[:, :, columns(seq_index)], here.at[0]
+    )
+    mine.start()
+    own[slot(0)] = x_ref[dp_index]
+    for c in range(1, seq_count):
+        v_copies[c - 1].wait_recv()
+        g_copies.append(gather(c))
+    for c in range(seq_count):
+        v_out[:, columns(lax.rem(seq_index + seq_count - c, seq_count))] = gathered[c, slot(0)]
+    for copy in x_copies:
+        copy.wait_recv()
+
+    t_copies = []
+    for c in range(seq_count):
+        for copy in g_copies[c]:
+            copy.wait_recv()
+        term = lax.dot_general(
+            own[...], gathered[c], (((0,), (0,)), ((), ())), preferred_element_type=jnp.float32
+        )
+        rows = term.shape[0] // seq_count
+        for j in range(seq_count):
+            terms[c, j] = term[j * rows : (j + 1) * rows].astype(jnp.bfloat16)
+        sends = [
+            to_seq(
+                terms.at[c, seq_peer(e)], arrived.at[e, c], t_send.at[e, c], t_recv.at[e, c], e
+            )
+            for e in range(1, seq_count)
+        ]
+        for copy in sends:
+            copy.start()
+        t_copies.append(sends)
+
+    for k in range(seq_count):
+        total = terms[k, seq_index].astype(jnp.float32)
+        for e in range(1, seq_count):
+            c = (k - e) % seq_count
+            t_copies[c][e - 1].wait_recv()
+            total += arrived[e, c].astype(jnp.float32)
+        w_out[:, columns(lax.rem(seq_index + seq_count - k, seq_count))] = total
+    mine.wait()
+    for copy in qk_copies:
+        copy.wait_recv()
+    for copy in v_copies + x_copies + qk_copies:
+        copy.wait_send()
+    for copies in g_copies + t_copies:
+        for copy in copies:
+            copy.wait_send()
+
+
+def return_grads(v_grad, qk_grad, inputs):
+    seq_count, tokens, group = v_grad.shape
+    dp_count, _, rows_block = inputs.shape
+    width = seq_count * group
+    rows = rows_block // seq_count
+    vmem = pl.BlockSpec(memory_space=pltpu.VMEM)
+
+    def pair(*shape):
+        return [pltpu.SemaphoreType.DMA(shape), pltpu.SemaphoreType.DMA(shape)]
+
+    return pl.pallas_call(
+        functools.partial(return_kernel, seq_count, dp_count),
+        in_specs=[vmem] * 3,
+        out_specs=[vmem] * 3,
+        out_shape=[
+            jax.ShapeDtypeStruct((2, tokens, width), jnp.bfloat16),
+            jax.ShapeDtypeStruct((tokens, width), jnp.bfloat16),
+            jax.ShapeDtypeStruct((rows, width), jnp.float32),
+        ],
+        scratch_shapes=[
+            pltpu.VMEM((dp_count * tokens, rows_block), jnp.bfloat16),
+            pltpu.VMEM((seq_count, dp_count * tokens, group), jnp.bfloat16),
+            pltpu.VMEM((seq_count, seq_count, rows, group), jnp.bfloat16),
+            pltpu.VMEM((seq_count, seq_count, rows, group), jnp.bfloat16),
+        ]
+        + pair(dp_count)
+        + pair(seq_count)
+        + pair(seq_count)
+        + pair(seq_count, dp_count)
+        + pair(seq_count, seq_count)
+        + [pltpu.SemaphoreType.DMA((1,))],
+        compiler_params=pltpu.CompilerParams(
+            collective_id=0, has_side_effects=True, vmem_limit_bytes=40 * 2**20
+        ),
+        cost_estimate=pl.CostEstimate(
+            flops=2 * dp_count * tokens * rows_block * width,
+            bytes_accessed=8 * tokens * width * dp_count,
+            transcendentals=0,
+        ),
+    )(v_grad, qk_grad, inputs)
 
 
 def per_device(
@@ -122,8 +292,6 @@
     qkv = lax.all_to_all(qkv, "seq", split_axis=0, concat_axis=0, tiled=True)
     rows_block = model // dp_count
     inputs = block_input[0].reshape(tokens, dp_count, rows_block).transpose(1, 0, 2)
-    inputs = lax.all_to_all(inputs, "dp", split_axis=0, concat_axis=0, tiled=True)
-    inputs = inputs.reshape(dp_count * tokens, rows_block)
 
     wide_grad = jnp.concatenate([low[:, :, :2], output_grad, high[:, :, :2]], axis=2)
     wide_pre = jnp.concatenate([low[:, :, 2:], pre_activation, high[:, :, 2:]], axis=2)
@@ -143,6 +311,7 @@
         .transpose(0, 2, 1, 3, 4)
         .reshape(1, patch_rows * patch_cols, 4 * channels)
     )
+    qkv, patches = lax.optimization_barrier((qkv, patches))
     patches = jnp.broadcast_to(patches, (seq_count,) + patches.shape[1:])
     patches = lax.all_to_all(patches, "seq", split_axis=0, concat_axis=0, tiled=True)
     patches = (
@@ -159,19 +328,7 @@
     ).astype(jnp.bfloat16)
 
     qk_grad, v_grad = attention_backward(qkv, attn_grad)
-    v_grad = lax.all_to_all(v_grad, "seq", split_axis=0, concat_axis=0, tiled=True)
-    value_grad = v_grad.transpose(1, 0, 2).reshape(tokens, width)
-    values = lax.all_gather(value_grad, "dp", axis=0, tiled=True)
-    qk_grad = lax.all_to_all(qk_grad, "seq", split_axis=0, concat_axis=0, tiled=True)
-    qk_grad = qk_grad.transpose(1, 2, 0, 3).reshape(2, tokens, width)
-    term = lax.dot_general(
-        inputs, values, (((0,), (0,)), ((), ())), preferred_element_type=jnp.float32
-    ).astype(jnp.bfloat16)
-    terms = lax.all_to_all(
-        term.reshape(seq_count, rows_block // seq_count, width),
-        "seq", split_axis=0, concat_axis=0, tiled=True,
-    )
-    weight_grad = jnp.sum(terms.astype(jnp.float32), axis=0)
+    qk_grad, value_grad, weight_grad = return_grads(v_grad, qk_grad, inputs)
     return (qk_grad[:1], qk_grad[1:], value_grad[None], weight_grad)
 
 

time: 210 us -> 155 us (0.74)
  waiting for transfers between devices: 81 us -> 6.59 us
  Pallas kernels: 7.33 us -> 78 us
  blocking collectives: 38.2 us -> 0 us
  matrix products: 19 us -> 34 us
  between operations: 15 us -> 1.61 us
  starting transfers between devices: 23.9 us -> 16.9 us
  local copies, waits for them, and re-layouts: 20.1 us -> 14.6 us
    pallas_call x0 -> x1, Pallas kernels: none -> 71.1 us  [return_grads(): pl.pallas_call(functools.partial(return_kernel, seq_count, dp_count), in_...]
    all_to_all x2 -> x0, blocking collectives: 38.2 us -> none  [the longest x1 21.7 us: per_device(): lax.all_to_all(inputs, 'dp', split_axis=0, concat_axis=0, tiled=True)]
    all_to_all x2 -> x0, waiting for transfers between devices: 35.1 us -> none  [the longest x1 30.6 us: per_device(): lax.all_to_all(term.reshape(seq_count, rows_block // seq_count, width), '...]
    all_to_all x1, waiting for transfers between devices: 27.2 us -> 2.36 us  [per_device(): qkv = lax.all_to_all(qkv, 'seq', split_axis=0, concat_axis=0, tiled=True)]
    conv_general_dilated x2, matrix products: 9.29 us -> 29.5 us  [conv_grad(): lax.conv_general_dilated(grad, flipped, (1, 1), (rows_pad, (0, 0)), dimen...]
    all_gather x1 -> x0, waiting for transfers between devices: 14.6 us -> none  [per_device(): values = lax.all_gather(value_grad, 'dp', axis=0, tiled=True)]
    all_to_all x2 -> x0, starting transfers between devices: 7.27 us -> none  [the longest x1 3.69 us: per_device(): lax.all_to_all(term.reshape(seq_count, rows_block // seq_count, width), '...]
    dot_general x1 -> x0, matrix products: 5.21 us -> none  [per_device(): lax.dot_general(inputs, values, (((0,), (0,)), ((), ())), preferred_eleme...]
  transfers between devices with their start and end apart: 7 -> 4, of which waited for: 5 -> 2; matrix products, arithmetic and copies ran while one was open for 11% -> 25% of each run, Pallas kernels for 0% -> 0%
where the time goes in v2:
time: 155 us; the launch traced here: 154 us
  Pallas kernels  78 us (50%)
  matrix products  34 us (22%)
  starting transfers between devices  16.9 us (11%)
  local copies, waits for them, and re-layouts  14.6 us (9%)
  waiting for transfers between devices  6.59 us (4%)
  other arithmetic  2.56 us (2%)
  between operations  1.61 us (1%)
    pallas_call x1, Pallas kernels, return_grads(): pl.pallas_call(functools.partial(return_kernel, seq_count, dp_count), in_...  71.1 us
    conv_general_dilated x2, matrix products, conv_grad(): lax.conv_general_dilated(grad, flipped, (1, 1), (rows_pad, (0, 0)), dimen...  29.5 us
    pallas_call x1, Pallas kernels, attention_backward(): pl.pallas_call(head_kernel, grid=(heads,), in_specs=[part(0), part(1), pa...  6.88 us
    all_to_all x1, starting transfers between devices, per_device(): qkv = lax.all_to_all(qkv, 'seq', split_axis=0, concat_axis=0, tiled=True)  6.08 us
    unnamed x29, local copies, waits for them, and re-layouts  6.02 us
    ppermute x1, starting transfers between devices, per_device(): lax.ppermute(jnp.concatenate([output_grad[:, :, -2:], pre_activation[:, :...  5.68 us
    dot_general x1, matrix products, per_device(): lax.dot_general(branch_grad, group_weight, (((1,), (1,)), ((), ())), pref...  4.47 us
    all_to_all x1, waiting for transfers between devices, per_device(): lax.all_to_all(patches, 'seq', split_axis=0, concat_axis=0, tiled=True)  4.22 us
  transfers between devices with their start and end apart: 4, of which 2 were waited for; matrix products, arithmetic and copies ran while one was open for 25% of the time, Pallas kernels for 0%

profile of v2, /device:TPU:0, one launch (start us, length us, event | category | flops | bytes accessed | tf_op | source)
XLA Modules:
  0.0 154.3 jit_solution(776927781127204165)
XLA Ops:
  0.6 0.0 copy-start
  0.6 0.0 copy-start.5
  0.7 2.1 %copy.55 = bf16[1,16,32,512]{3,0,2,1:T(2,128)(2,1)S(1)} copy(bf16[1,16,32,512]{3,2,1,0:T(8,128)(2,1)} %param.13) | data formatting | bytes 1048576 | tf_op args[1]
  2.8 0.0 copy-start.1
  2.8 0.0 copy-start.6
  2.8 0.1 fusion.12
  3.0 0.0 copy-done.5
  3.0 1.0 copy.56
  3.9 0.0 copy-start.3
  4.0 0.0 copy-start.7
  4.0 0.1 fusion.13
  4.0 0.8 pad_maximum_fusion.3
  4.8 5.7 %collective-permute-start = (bf16[1,16,3,512]{3,0,2,1:T(2,128)(2,1)}, bf16[1,16,3,512]{3,0,2,1:T(2,128)(2,1)}, u32[]{:S(2)}, u32[]{:S(2)}) collective-permute-start(bf16[1,16,3,512]{3,0,2,1:T(2,128)(2,1)} %pad_maximum_fusion.3), channel_id=1, source_target_pairs={{0,1},{1,2},{2,3},{4,5},{5,6},{6,7},{8,9},{9,10},{10,11},{12,13},{... | collective-permute-start | bytes 147464 | tf_op jit(solution)/shard_map/ppermute | solution.py:284
  10.5 0.8 pad_maximum_fusion.4
  11.3 1.3 collective-permute-start.1
  12.6 0.3 copy.51
  12.9 0.3 copy.52
  13.2 0.3 copy.53
  13.4 0.2 pad_maximum_fusion
  13.6 1.6 %copy.54 = bf16[3,128,4,512]{3,1,0,2:T(8,128)(2,1)} copy(bf16[3,128,4,512]{1,3,2,0:T(8,128)(2,1)S(1)} %bitcast.29) | data formatting | bytes 3145728 | tf_op jit(solution)/shard_map/reshape | solution.py:291
  15.2 6.1 %all-to-all-start = ((bf16[4,3,128,512]{3,2,1,0:T(8,128)(2,1)}), bf16[4,3,128,512]{3,2,1,0:T(8,128)(2,1)S(1)}, u32[]{:S(2)}, u32[]{:S(2)}) async-start(bf16[4,3,128,512]{3,2,1,0:T(8,128)(2,1)} %bitcast.1), calls=%async_computation | async-start | bytes 3145728 | tf_op jit(solution)/shard_map/all_to_all | solution.py:292
  22.0 0.0 collective-permute-done
  22.0 0.9 slice.42
  22.9 0.8 slice.46
  23.7 0.0 collective-permute-done.1
  23.7 0.9 slice.45
  24.6 0.8 slice.47
  25.4 0.0 copy-start.9
  25.5 25.2 %fusion.2 = bf16[1,16,34,512]{3,0,2,1:T(2,128)(2,1)S(1)} fusion(bf16[3,3,512,512]{3,2,1,0:T(8,128)(2,1)} %param.14, pred[34]{0:T(512)(128)(4,1)S(1)} %or_and_fusion, bf16[1,16,2,512]{3,0,2,1:T(2,128)(2,1)S(1)} %slice.45, bf16[1,16,32,512]{3,0,2,1:T(2,128)(2,1)S(1)} %copy-done.2, bf16[1,16,2,512]{3,0,2,1:T(2,128)(2,1)S(1)} %slice.42, ...), kind=kOutput, calls=%fused_computation.6 | convolution fusion | flops 2465349632 | bytes 6422562 | tf_op jit(solution)/shard_map/conv_general_dilated | solution.py:20
  50.6 0.0 copy-done.9
  50.6 4.4 %convolution_convert_fusion = bf16[1,16,32,16]{3,0,2,1:T(2,128)(2,1)S(1)} fusion(bf16[1,16,34,512]{3,0,2,1:T(2,128)(2,1)S(1)} %fusion.2, bf16[3,3,16,512]{3,2,1,0:T(8,128)(2,1)S(1)} %copy-done.9), kind=kOutput, calls=%fused_computation.12 | convolution fusion | flops 72359936 | bytes 720896 | tf_op jit(solution)/shard_map/conv_general_dilated | solution.py:20
  55.0 0.0 copy-start.4
  55.1 0.2 copy.61
  55.2 0.1 reshape.108
  55.4 2.4 %all-to-all-done.q_ref.k_ref.v_ref = bf16[4,3,128,512]{3,2,1,0:T(8,128)(2,1)S(1)} async-done(((bf16[4,3,128,512]{3,2,1,0:T(8,128)(2,1)}), bf16[4,3,128,512]{3,2,1,0:T(8,128)(2,1)S(1)}, u32[]{:S(2)}, u32[]{:S(2)}) %all-to-all-start) | async-done | bytes 1572896 | tf_op jit(solution)/shard_map/all_to_all | solution.py:292
  57.7 0.6 broadcast_in_dim.26
  58.4 3.9 %all-to-all-start.1 = ((bf16[4,128,64]{1,2,0:T(8,128)(2,1)}), bf16[4,128,64]{1,2,0:T(8,128)(2,1)}, u32[]{:S(2)}, u32[]{:S(2)}) async-start(bf16[4,128,64]{1,2,0:T(8,128)(2,1)} %broadcast_in_dim.26), calls=%async_computation.1 | async-start | bytes 131072 | tf_op jit(solution)/shard_map/all_to_all | solution.py:316
  62.3 0.8 dynamic-slice_convert_fusion
  63.1 0.4 copy.64
  63.5 0.4 copy.65
  63.9 4.2 %all-to-all-done.1 = bf16[4,128,64]{1,2,0:T(8,128)(2,1)} async-done(((bf16[4,128,64]{1,2,0:T(8,128)(2,1)}), bf16[4,128,64]{1,2,0:T(8,128)(2,1)}, u32[]{:S(2)}, u32[]{:S(2)}) %all-to-all-start.1) | async-done | bytes 65568 | tf_op jit(solution)/shard_map/all_to_all | solution.py:316
  68.1 1.0 copy.62
  69.1 4.5 %fusion.3.g_ref = bf16[512,512]{1,0:T(8,128)(2,1)S(1)} fusion(bf16[2048,3072]{1,0:T(8,128)(2,1)} %param.22, s32[]{:T(128)S(6)} %select_n.12, bf16[512,64]{1,0:T(8,128)(2,1)S(1)} %bitcast.33, bf16[64,3072]{1,0:T(8,128)(2,1)S(1)} %copy-done, f32[3072]{0:T(1024)S(1)} %bitcast.35), kind=kOutput, calls=%fused_computation.7 | convolution fusion | flops 1815347200 | bytes 4141060 | tf_op jit(solution)/shard_map/dot_general | solution.py:326
  73.5 6.9 %shard_map.147 = (bf16[4,2,128,512]{3,2,1,0:T(8,128)(2,1)S(1)}, bf16[4,128,512]{2,1,0:T(8,128)(2,1)S(1)}) custom-call(bf16[4,3,128,512]{3,2,1,0:T(8,128)(2,1)S(1)} %all-to-all-done.q_ref.k_ref.v_ref, bf16[4,3,128,512]{3,2,1,0:T(8,128)(2,1)S(1)} %all-to-all-done.q_ref.k_ref.v_ref, bf16[4,3,128,512]{3,2,1,0:T(8,128)(2,1)S(1)} %all-to-all-done.q_ref.k_ref.v_ref, ...), custom_call_target="tpu_custom_call" | custom-call | flops 1879048192 | bytes 3670016 | tf_op jit(solution)/shard_map/pallas_call | solution.py:71
  80.4 71.1 %shard_map.148 = (bf16[2,128,2048]{2,1,0:T(8,128)(2,1)S(1)}, bf16[128,2048]{1,0:T(8,128)(2,1)S(1)}, f32[96,2048]{1,0:T(8,128)S(1)}) custom-call(bf16[4,128,512]{2,1,0:T(8,128)(2,1)S(1)} %get-tuple-element.13.v_ref, bf16[4,2,128,512]{3,2,1,0:T(8,128)(2,1)S(1)} %get-tuple-element.14.qk_ref, bf16[8,128,384]{2,1,0:T(8,128)(2,1)S(1)} %bitcast.27), custom_call_target="tpu_custom_call" | custom-call | flops 1610612736 | bytes 16777216 | tf_op jit(solution)/shard_map/pallas_call | solution.py:228
  151.6 1.1 fusion.11
  152.7 0.8 copy.70
  153.5 0.9 copy.71
  (13 shorter events, 0.1 us)
Async XLA Ops:
  0.6 68.4 %copy-start = (bf16[64,3072]{1,0:T(8,128)(2,1)S(1)}, bf16[64,3072]{1,0:T(8,128)(2,1)}, u32[]{:S(2)}) copy-start(bf16[64,3072]{1,0:T(8,128)(2,1)} %param.16) | copy-start | bytes 1179652
  0.6 2.3 %copy-start.5 = (bf16[1,16,32,512]{3,2,1,0:T(8,128)(2,1)S(1)}, bf16[1,16,32,512]{3,2,1,0:T(8,128)(2,1)}, u32[]{:S(2)}) copy-start(bf16[1,16,32,512]{3,2,1,0:T(8,128)(2,1)} %param.12) | copy-start | bytes 1572868
  2.8 8.5 %copy-start.1 = (bf16[1,16,32,512]{3,0,2,1:T(2,128)(2,1)}, bf16[1,16,32,512]{3,0,2,1:T(2,128)(2,1)S(1)}, u32[]{:S(2)}) copy-start(bf16[1,16,32,512]{3,0,2,1:T(2,128)(2,1)S(1)} %copy.55) | copy-start | bytes 1572868
  2.8 9.8 %copy-start.6 = (bf16[1,128,2048]{2,1,0:T(8,128)(2,1)S(1)}, bf16[1,128,2048]{2,1,0:T(8,128)(2,1)}, u32[]{:S(2)}) copy-start(bf16[1,128,2048]{2,1,0:T(8,128)(2,1)} %param.19) | copy-start | bytes 1572868
  3.9 7.3 %copy-start.3 = (bf16[1,16,32,512]{3,0,2,1:T(2,128)(2,1)}, bf16[1,16,32,512]{3,0,2,1:T(2,128)(2,1)S(1)}, u32[]{:S(2)}) copy-start(bf16[1,16,32,512]{3,0,2,1:T(2,128)(2,1)S(1)} %copy.56) | copy-start | bytes 1572868
  4.0 8.9 %copy-start.7 = (bf16[1,128,2048]{2,1,0:T(8,128)(2,1)S(1)}, bf16[1,128,2048]{2,1,0:T(8,128)(2,1)}, u32[]{:S(2)}) copy-start(bf16[1,128,2048]{2,1,0:T(8,128)(2,1)} %param.20) | copy-start | bytes 1572868
  4.8 8.3 %copy-start.8 = (bf16[1,128,2048]{2,1,0:T(8,128)(2,1)S(1)}, bf16[1,128,2048]{2,1,0:T(8,128)(2,1)}, u32[]{:S(2)}) copy-start(bf16[1,128,2048]{2,1,0:T(8,128)(2,1)} %param.21) | copy-start | bytes 1572868
  4.8 17.2 %collective-permute-start = (bf16[1,16,3,512]{3,0,2,1:T(2,128)(2,1)}, bf16[1,16,3,512]{3,0,2,1:T(2,128)(2,1)}, u32[]{:S(2)}, u32[]{:S(2)}) collective-permute-start(bf16[1,16,3,512]{3,0,2,1:T(2,128)(2,1)} %pad_maximum_fusion.3), channel_id=1, source_target_pairs={{0,1},{1,2},{2,3},{4,5},{5,6},{6,7},{8,9},{9,10},{10,11},{12,13},{... | collective-permute-start | bytes 147464 | tf_op jit(solution)/shard_map/ppermute | solution.py:284
  11.3 12.4 %collective-permute-start.1 = (bf16[1,16,3,512]{3,0,2,1:T(2,128)(2,1)}, bf16[1,16,3,512]{3,0,2,1:T(2,128)(2,1)}, u32[]{:S(2)}, u32[]{:S(2)}) collective-permute-start(bf16[1,16,3,512]{3,0,2,1:T(2,128)(2,1)} %pad_maximum_fusion.4), channel_id=1, source_target_pairs={{1,0},{2,1},{3,2},{5,4},{6,5},{7,6},{9,8},{10,9},{11,10},{13,12},{... | collective-permute-start | bytes 147464 | tf_op jit(solution)/shard_map/ppermute | solution.py:287
  15.2 10.2 %copy-start.2 = (bf16[1,16,32,512]{3,0,2,1:T(2,128)(2,1)S(1)}, bf16[1,16,32,512]{3,0,2,1:T(2,128)(2,1)}, u32[]{:S(2)}) copy-start(bf16[1,16,32,512]{3,0,2,1:T(2,128)(2,1)} %copy-done.1) | copy-start | bytes 1572868
  15.2 42.5 %all-to-all-start = ((bf16[4,3,128,512]{3,2,1,0:T(8,128)(2,1)}), bf16[4,3,128,512]{3,2,1,0:T(8,128)(2,1)S(1)}, u32[]{:S(2)}, u32[]{:S(2)}) async-start(bf16[4,3,128,512]{3,2,1,0:T(8,128)(2,1)} %bitcast.1), calls=%async_computation | async-start | bytes 3145728 | tf_op jit(solution)/shard_map/all_to_all | solution.py:292
  25.4 25.2 %copy-start.9 = (bf16[3,3,16,512]{3,2,1,0:T(8,128)(2,1)S(1)}, bf16[3,3,16,512]{3,2,1,0:T(8,128)(2,1)}, u32[]{:S(2)}) copy-start(bf16[3,3,16,512]{3,2,1,0:T(8,128)(2,1)} %param.15) | copy-start | bytes 442372
  55.0 8.1 %copy-start.4 = (bf16[1,128,3072]{2,1,0:T(8,128)(2,1)S(1)}, bf16[1,128,3072]{2,1,0:T(8,128)(2,1)}, u32[]{:S(2)}) copy-start(bf16[1,128,3072]{2,1,0:T(8,128)(2,1)} %param.23) | copy-start | bytes 2359300
  58.4 9.7 %all-to-all-start.1 = ((bf16[4,128,64]{1,2,0:T(8,128)(2,1)}), bf16[4,128,64]{1,2,0:T(8,128)(2,1)}, u32[]{:S(2)}, u32[]{:S(2)}) async-start(bf16[4,128,64]{1,2,0:T(8,128)(2,1)} %broadcast_in_dim.26), calls=%async_computation.1 | async-start | bytes 131072 | tf_op jit(solution)/shard_map/all_to_all | solution.py:316

commit v3 on v2

--- a/solution.py
+++ b/solution.py
@@ -296,6 +296,7 @@
     wide_grad = jnp.concatenate([low[:, :, :2], output_grad, high[:, :, :2]], axis=2)
     wide_pre = jnp.concatenate([low[:, :, 2:], pre_activation, high[:, :, 2:]], axis=2)
     act_grad = conv_grad(wide_grad, up_kernel, (1, 1))
+    act_grad = lax.optimization_barrier(act_grad)
     columns = jnp.arange(wide_pre.shape[2])
     inside = ((columns > 0) | (seq_index > 0)) & (
         (columns < wide_pre.shape[2] - 1) | (seq_index < seq_count - 1)

time: 155 us -> 155 us (level)
  matrix products: 34 us -> 28.7 us
  waiting for transfers between devices: 6.59 us -> 9.67 us
  local copies, waits for them, and re-layouts: 14.6 us -> 16.2 us
    conv_general_dilated x2, matrix products: 29.5 us -> 24.2 us  [conv_grad(): lax.conv_general_dilated(grad, flipped, (1, 1), (rows_pad, (0, 0)), dimen...]
    all_to_all x1, waiting for transfers between devices: 2.36 us -> 5.44 us  [per_device(): qkv = lax.all_to_all(qkv, 'seq', split_axis=0, concat_axis=0, tiled=True)]
    unnamed x29 -> x23, local copies, waits for them, and re-layouts: 6.02 us -> 7.14 us
  transfers between devices with their start and end apart: 4 -> 4, of which waited for: 2 -> 2; matrix products, arithmetic and copies ran while one was open for 25% -> 24% of each run, Pallas kernels for 0% -> 0%
where the time goes in v3:
time: 155 us
  Pallas kernels  78 us (50%)
  matrix products  28.7 us (19%)
  starting transfers between devices  16.6 us (11%)
  local copies, waits for them, and re-layouts  16.2 us (10%)
  waiting for transfers between devices  9.67 us (6%)
  other arithmetic  3.84 us (2%)
  between operations  1.56 us (1%)
    pallas_call x1, Pallas kernels, return_grads(): pl.pallas_call(functools.partial(return_kernel, seq_count, dp_count), in_...  71.1 us
    conv_general_dilated x2, matrix products, conv_grad(): lax.conv_general_dilated(grad, flipped, (1, 1), (rows_pad, (0, 0)), dimen...  24.2 us
    unnamed x23, local copies, waits for them, and re-layouts  7.14 us
    pallas_call x1, Pallas kernels, attention_backward(): pl.pallas_call(head_kernel, grid=(heads,), in_specs=[part(0), part(1), pa...  6.88 us
    all_to_all x1, starting transfers between devices, per_device(): qkv = lax.all_to_all(qkv, 'seq', split_axis=0, concat_axis=0, tiled=True)  5.94 us
    ppermute x1, starting transfers between devices, per_device(): lax.ppermute(jnp.concatenate([output_grad[:, :, -2:], pre_activation[:, :...  5.54 us
    all_to_all x1, waiting for transfers between devices, per_device(): qkv = lax.all_to_all(qkv, 'seq', split_axis=0, concat_axis=0, tiled=True)  5.44 us
    dot_general x1, matrix products, per_device(): lax.dot_general(branch_grad, group_weight, (((1,), (1,)), ((), ())), pref...  4.47 us
  transfers between devices with their start and end apart: 4, of which 2 were waited for; matrix products, arithmetic and copies ran while one was open for 24% of the time, Pallas kernels for 0%

profile of v3, /device:TPU:0, one launch (start us, length us, event | category | flops | bytes accessed | tf_op | source)
XLA Modules:
  0.0 154.6 jit_solution(1267290015494568448)
XLA Ops:
  0.6 0.0 copy-start
  0.6 0.0 copy-start.2
  0.7 0.0 copy-start.3
  0.7 1.4 copy.71
  2.1 1.0 fusion.18
  3.2 0.0 copy-start.4
  3.2 0.6 pad_maximum_fusion.3
  3.8 5.5 %collective-permute-start = (bf16[1,16,3,512]{3,1,2,0:T(8,128)(2,1)}, bf16[1,16,3,512]{3,1,2,0:T(8,128)(2,1)}, u32[]{:S(2)}, u32[]{:S(2)}) collective-permute-start(bf16[1,16,3,512]{3,1,2,0:T(8,128)(2,1)} %pad_maximum_fusion.3), channel_id=1, source_target_pairs={{0,1},{1,2},{2,3},{4,5},{5,6},{6,7},{8,9},{9,10},{10,11},{12,13},{... | collective-permute-start | bytes 147464 | tf_op jit(solution)/shard_map/ppermute | solution.py:284
  9.4 0.6 pad_maximum_fusion.4
  10.0 1.3 collective-permute-start.1
  11.3 0.0 copy-done.2
  11.3 0.3 copy.66
  11.6 0.3 copy.67
  11.8 0.0 copy-done.4
  11.8 1.0 copy.68
  12.8 1.2 pad_maximum_fusion
  14.1 1.6 %copy.69 = bf16[3,128,4,512]{3,1,0,2:T(8,128)(2,1)} copy(bf16[3,128,4,512]{1,3,2,0:T(8,128)(2,1)S(1)} %bitcast.28) | data formatting | bytes 3145728 | tf_op jit(solution)/shard_map/reshape | solution.py:291
  15.7 5.9 %all-to-all-start = ((bf16[4,3,128,512]{3,2,1,0:T(8,128)(2,1)}), bf16[4,3,128,512]{3,2,1,0:T(8,128)(2,1)S(1)}, u32[]{:S(2)}, u32[]{:S(2)}) async-start(bf16[4,3,128,512]{3,2,1,0:T(8,128)(2,1)} %bitcast.1), calls=%async_computation | async-start | bytes 3145728 | tf_op jit(solution)/shard_map/all_to_all | solution.py:292
  21.6 2.0 %copy.75 = bf16[1,16,32,512]{3,0,2,1:T(2,128)(2,1)S(1)} copy(bf16[1,16,32,512]{3,2,1,0:T(8,128)(2,1)} %param.13) | data formatting | bytes 1048576 | tf_op args[1]
  24.3 0.0 collective-permute-done
  24.3 0.8 slice.41
  25.1 0.1 copy.74
  25.2 0.0 collective-permute-done.1
  25.2 0.8 slice.43
  25.9 0.1 copy.76
  26.0 20.2 %fusion.5 = f32[1,16,34,512]{3,0,2,1:T(1,128)S(1)} fusion(bf16[3,3,512,512]{3,2,1,0:T(8,128)(2,1)} %param.14, bf16[1,16,2,512]{3,0,2,1:T(2,128)(2,1)S(1)} %copy.76, bf16[1,16,32,512]{3,0,2,1:T(2,128)(2,1)S(1)} %copy.75, bf16[1,16,2,512]{3,0,2,1:T(2,128)(2,1)S(1)} %copy.74), kind=kOutput, calls=%fused_computation.8 | convolution fusion | flops 2461728768 | bytes 6422528 | tf_op jit(solution)/shard_map/conv_general_dilated | solution.py:20
  46.2 0.0 copy-start.5
  46.2 0.8 slice.44
  47.0 0.7 slice.45
  47.7 0.5 fusion.13
  48.2 4.0 %convolution_convert_fusion = bf16[1,16,32,16]{3,0,2,1:T(2,128)(2,1)S(1)} fusion(bf16[3,3,16,512]{3,2,1,0:T(8,128)(2,1)S(1)} %copy-done.5, bf16[1,16,34,512]{3,1,2,0:T(8,128)(2,1)S(1)} %fusion.13), kind=kOutput, calls=%fused_computation.9 | convolution fusion | flops 72359936 | bytes 720896 | tf_op jit(solution)/shard_map/conv_general_dilated | solution.py:20
  52.2 0.0 copy-start.1
  52.3 0.2 copy.80
  52.4 0.1 reshape.108
  52.6 5.4 %all-to-all-done.q_ref.k_ref.v_ref = bf16[4,3,128,512]{3,2,1,0:T(8,128)(2,1)S(1)} async-done(((bf16[4,3,128,512]{3,2,1,0:T(8,128)(2,1)}), bf16[4,3,128,512]{3,2,1,0:T(8,128)(2,1)S(1)}, u32[]{:S(2)}, u32[]{:S(2)}) %all-to-all-start) | async-done | bytes 1572896 | tf_op jit(solution)/shard_map/all_to_all | solution.py:292
  58.0 0.6 broadcast_in_dim.26
  58.7 3.9 %all-to-all-start.1 = ((bf16[4,128,64]{1,2,0:T(8,128)(2,1)}), bf16[4,128,64]{1,2,0:T(8,128)(2,1)}, u32[]{:S(2)}, u32[]{:S(2)}) async-start(bf16[4,128,64]{1,2,0:T(8,128)(2,1)} %broadcast_in_dim.26), calls=%async_computation.1 | async-start | bytes 131072 | tf_op jit(solution)/shard_map/all_to_all | solution.py:317
  62.6 0.8 dynamic-slice_convert_fusion
  63.4 0.4 copy.83
  63.8 0.4 copy.84
  64.1 4.2 %all-to-all-done.1 = bf16[4,128,64]{1,2,0:T(8,128)(2,1)} async-done(((bf16[4,128,64]{1,2,0:T(8,128)(2,1)}), bf16[4,128,64]{1,2,0:T(8,128)(2,1)}, u32[]{:S(2)}, u32[]{:S(2)}) %all-to-all-start.1) | async-done | bytes 65568 | tf_op jit(solution)/shard_map/all_to_all | solution.py:317
  68.4 1.0 copy.81
  69.4 4.5 %fusion.2.g_ref = bf16[512,512]{1,0:T(8,128)(2,1)S(1)} fusion(bf16[2048,3072]{1,0:T(8,128)(2,1)} %param.22, s32[]{:T(128)S(6)} %select_n.12, bf16[512,64]{1,0:T(8,128)(2,1)S(1)} %bitcast.32, bf16[64,3072]{1,0:T(8,128)(2,1)S(1)} %copy-done, f32[3072]{0:T(1024)S(1)} %bitcast.34), kind=kOutput, calls=%fused_computation.6 | convolution fusion | flops 1815347200 | bytes 4141060 | tf_op jit(solution)/shard_map/dot_general | solution.py:327
  73.8 6.9 %shard_map.147 = (bf16[4,2,128,512]{3,2,1,0:T(8,128)(2,1)S(1)}, bf16[4,128,512]{2,1,0:T(8,128)(2,1)S(1)}) custom-call(bf16[4,3,128,512]{3,2,1,0:T(8,128)(2,1)S(1)} %all-to-all-done.q_ref.k_ref.v_ref, bf16[4,3,128,512]{3,2,1,0:T(8,128)(2,1)S(1)} %all-to-all-done.q_ref.k_ref.v_ref, bf16[4,3,128,512]{3,2,1,0:T(8,128)(2,1)S(1)} %all-to-all-done.q_ref.k_ref.v_ref, ...), custom_call_target="tpu_custom_call" | custom-call | flops 1879048192 | bytes 3670016 | tf_op jit(solution)/shard_map/pallas_call | solution.py:71
  80.7 71.1 %shard_map.148 = (bf16[2,128,2048]{2,1,0:T(8,128)(2,1)S(1)}, bf16[128,2048]{1,0:T(8,128)(2,1)S(1)}, f32[96,2048]{1,0:T(8,128)S(1)}) custom-call(bf16[4,128,512]{2,1,0:T(8,128)(2,1)S(1)} %get-tuple-element.13.v_ref, bf16[4,2,128,512]{3,2,1,0:T(8,128)(2,1)S(1)} %get-tuple-element.14.qk_ref, bf16[8,128,384]{2,1,0:T(8,128)(2,1)S(1)} %bitcast.26), custom_call_target="tpu_custom_call" | custom-call | flops 1610612736 | bytes 16777216 | tf_op jit(solution)/shard_map/pallas_call | solution.py:228
  151.9 1.1 fusion.17
  152.9 0.8 copy.94
  153.7 0.9 copy.95
  (10 shorter events, 0.1 us)
Async XLA Ops:
  0.6 68.7 %copy-start = (bf16[64,3072]{1,0:T(8,128)(2,1)S(1)}, bf16[64,3072]{1,0:T(8,128)(2,1)}, u32[]{:S(2)}) copy-start(bf16[64,3072]{1,0:T(8,128)(2,1)} %param.16) | copy-start | bytes 1179652
  0.6 10.6 %copy-start.2 = (bf16[1,128,2048]{2,1,0:T(8,128)(2,1)S(1)}, bf16[1,128,2048]{2,1,0:T(8,128)(2,1)}, u32[]{:S(2)}) copy-start(bf16[1,128,2048]{2,1,0:T(8,128)(2,1)} %param.19) | copy-start | bytes 1572868
  0.7 10.9 %copy-start.3 = (bf16[1,128,2048]{2,1,0:T(8,128)(2,1)S(1)}, bf16[1,128,2048]{2,1,0:T(8,128)(2,1)}, u32[]{:S(2)}) copy-start(bf16[1,128,2048]{2,1,0:T(8,128)(2,1)} %param.20) | copy-start | bytes 1572868
  3.2 8.7 %copy-start.4 = (bf16[1,128,2048]{2,1,0:T(8,128)(2,1)S(1)}, bf16[1,128,2048]{2,1,0:T(8,128)(2,1)}, u32[]{:S(2)}) copy-start(bf16[1,128,2048]{2,1,0:T(8,128)(2,1)} %param.21) | copy-start | bytes 1572868
  3.8 20.5 %collective-permute-start = (bf16[1,16,3,512]{3,1,2,0:T(8,128)(2,1)}, bf16[1,16,3,512]{3,1,2,0:T(8,128)(2,1)}, u32[]{:S(2)}, u32[]{:S(2)}) collective-permute-start(bf16[1,16,3,512]{3,1,2,0:T(8,128)(2,1)} %pad_maximum_fusion.3), channel_id=1, source_target_pairs={{0,1},{1,2},{2,3},{4,5},{5,6},{6,7},{8,9},{9,10},{10,11},{12,13},{... | collective-permute-start | bytes 147464 | tf_op jit(solution)/shard_map/ppermute | solution.py:284
  10.0 15.2 %collective-permute-start.1 = (bf16[1,16,3,512]{3,1,2,0:T(8,128)(2,1)}, bf16[1,16,3,512]{3,1,2,0:T(8,128)(2,1)}, u32[]{:S(2)}, u32[]{:S(2)}) collective-permute-start(bf16[1,16,3,512]{3,1,2,0:T(8,128)(2,1)} %pad_maximum_fusion.4), channel_id=1, source_target_pairs={{1,0},{2,1},{3,2},{5,4},{6,5},{7,6},{9,8},{10,9},{11,10},{13,12},{... | collective-permute-start | bytes 147464 | tf_op jit(solution)/shard_map/ppermute | solution.py:287
  15.7 42.3 %all-to-all-start = ((bf16[4,3,128,512]{3,2,1,0:T(8,128)(2,1)}), bf16[4,3,128,512]{3,2,1,0:T(8,128)(2,1)S(1)}, u32[]{:S(2)}, u32[]{:S(2)}) async-start(bf16[4,3,128,512]{3,2,1,0:T(8,128)(2,1)} %bitcast.1), calls=%async_computation | async-start | bytes 3145728 | tf_op jit(solution)/shard_map/all_to_all | solution.py:292
  46.2 2.0 %copy-start.5 = (bf16[3,3,16,512]{3,2,1,0:T(8,128)(2,1)S(1)}, bf16[3,3,16,512]{3,2,1,0:T(8,128)(2,1)}, u32[]{:S(2)}) copy-start(bf16[3,3,16,512]{3,2,1,0:T(8,128)(2,1)} %param.15) | copy-start | bytes 442372
  52.2 11.1 %copy-start.1 = (bf16[1,128,3072]{2,1,0:T(8,128)(2,1)S(1)}, bf16[1,128,3072]{2,1,0:T(8,128)(2,1)}, u32[]{:S(2)}) copy-start(bf16[1,128,3072]{2,1,0:T(8,128)(2,1)} %param.23) | copy-start | bytes 2359300
  58.7 9.7 %all-to-all-start.1 = ((bf16[4,128,64]{1,2,0:T(8,128)(2,1)}), bf16[4,128,64]{1,2,0:T(8,128)(2,1)}, u32[]{:S(2)}, u32[]{:S(2)}) async-start(bf16[4,128,64]{1,2,0:T(8,128)(2,1)} %broadcast_in_dim.26), calls=%async_computation.1 | async-start | bytes 131072 | tf_op jit(solution)/shard_map/all_to_all | solution.py:317
